TPU v7x, 32 devices: a whole 2x2x4 slice. The times are simulated.
32 devices in a mesh: seq: 4 (over y, x), dp: 8 (over z, core).
Axes of the slice: x: 2, y: 2, z: 4, core: 2. Of those that a mesh axis runs over, the one named last changes fastest.
Arguments:
- inputs: bfloat16 [24, 512, 768], P('dp', 'seq'), may hold values from -6 to 6
- masked_positions: int32 [24, 76], P('dp'), may hold values from 0 to 511, as said below
- masked_grads: bfloat16 [24, 76, 768], P('dp'), may hold values from -6 to 6
- kernel_paths: int32 [24, 2], P('dp'), may hold values from 0 to 2, as said below
- attn_weight: float32 [2, 768, 2304], P(None, ('seq', 'dp')), may hold values from -0.21875 to 0.21875
- out_weight: float32 [2, 768, 768], P(None, ('seq', 'dp')), may hold values from -1.75 to 1.75
- point_weight: float32 [2, 768, 768], P(None, ('seq', 'dp')), may hold values from -0.21875 to 0.21875
- depth_weight: float32 [2, 7, 768], P(None, None, ('seq', 'dp')), may hold values from -2 to 2
- gains: float32 [2, 2, 768], P(None, None, ('seq', 'dp')), may hold values from 0.5 to 1.5
- shifts: float32 [2, 5, 768], P(None, None, ('seq', 'dp')), may hold values from -1.2 to 1.2
- first_attn: float32 [2, 768, 2304], P(None, ('seq', 'dp')), may hold values from -160 to 160
- first_out: float32 [2, 768, 768], P(None, ('seq', 'dp')), may hold values from -20 to 20
- first_point: float32 [2, 768, 768], P(None, ('seq', 'dp')), may hold values from -224 to 224
- first_depth: float32 [2, 7, 768], P(None, None, ('seq', 'dp')), may hold values from -320 to 320
- first_gains: float32 [2, 2, 768], P(None, None, ('seq', 'dp')), may hold values from -320 to 320
- first_shifts: float32 [2, 5, 768], P(None, None, ('seq', 'dp')), may hold values from -192 to 192
- second_attn: float32 [2, 768, 2304], P(None, ('seq', 'dp')), may hold values from 307.2 to 1228.8
- second_out: float32 [2, 768, 768], P(None, ('seq', 'dp')), may hold values from 6.144 to 24.576
- second_point: float32 [2, 768, 768], P(None, ('seq', 'dp')), may hold values from 614.4 to 2457.6
- second_depth: float32 [2, 7, 768], P(None, None, ('seq', 'dp')), may hold values from 1228.8 to 4915.2
- second_gains: float32 [2, 2, 768], P(None, None, ('seq', 'dp')), may hold values from 1228.8 to 4915.2
- second_shifts: float32 [2, 5, 768], P(None, None, ('seq', 'dp')), may hold values from 491.52 to 1966.08
Outputs:
- result: bfloat16 [24, 512, 768], P('dp', 'seq')
- input_grad: float32 [24, 512, 768], P('dp', 'seq')
- new_attn: float32 [2, 768, 2304], P(None, ('seq', 'dp'))
- new_out: float32 [2, 768, 768], P(None, ('seq', 'dp'))
- new_point: float32 [2, 768, 768], P(None, ('seq', 'dp'))
- new_depth: float32 [2, 7, 768], P(None, None, ('seq', 'dp'))
- new_gains: float32 [2, 2, 768], P(None, None, ('seq', 'dp'))
- new_shifts: float32 [2, 5, 768], P(None, None, ('seq', 'dp'))
- moment_attn: float32 [2, 768, 2304], P(None, ('seq', 'dp'))
- moment_out: float32 [2, 768, 768], P(None, ('seq', 'dp'))
- moment_point: float32 [2, 768, 768], P(None, ('seq', 'dp'))
- moment_depth: float32 [2, 7, 768], P(None, None, ('seq', 'dp'))
- moment_gains: float32 [2, 2, 768], P(None, None, ('seq', 'dp'))
- moment_shifts: float32 [2, 5, 768], P(None, None, ('seq', 'dp'))
- square_attn: float32 [2, 768, 2304], P(None, ('seq', 'dp'))
- square_out: float32 [2, 768, 768], P(None, ('seq', 'dp'))
- square_point: float32 [2, 768, 768], P(None, ('seq', 'dp'))
- square_depth: float32 [2, 7, 768], P(None, None, ('seq', 'dp'))
- square_gains: float32 [2, 2, 768], P(None, None, ('seq', 'dp'))
- square_shifts: float32 [2, 5, 768], P(None, None, ('seq', 'dp'))
- copy_attn: bfloat16 [2, 768, 2304], P(None, ('seq', 'dp'))
- copy_out: bfloat16 [2, 768, 768], P(None, ('seq', 'dp'))
- copy_point: bfloat16 [2, 768, 768], P(None, ('seq', 'dp'))
- copy_depth: bfloat16 [2, 7, 768], P(None, None, ('seq', 'dp'))
- copy_gains: bfloat16 [2, 2, 768], P(None, None, ('seq', 'dp'))
- copy_shifts: bfloat16 [2, 5, 768], P(None, None, ('seq', 'dp'))
Inputs may be any that keep to these rules, and one draw needn't show every extreme that they name: `masked_positions`: each row holds 76 distinct token positions of its sequence. Sequence s in block b uses a centred kernel of 2 kernel_paths[s, b] + 3 taps.
All inputs are finite; a program needn't handle non-finite values.
Results may differ from a plain program's by a relative error of at most 0.034.
Values may be sent and summed in bfloat16 or wider, within the bound.
No kernel may reach another device: no remote copies, remote signals or barrier semaphores. Data moves between devices by JAX's collectives and lax.ppermute only.
A program may use at most 192 MiB of HBM per device.

v0:
```python
from functools import partial

import jax
import jax.numpy as jnp
from jax import lax
from jax.sharding import PartitionSpec as P

HEADS = 12
STEP = 10


norm_eps = 1e-05
beta_first = 0.5
beta_second = 0.5
adam_eps = 1e-08
weight_decay = 0.01
rate_attn = 0.03
rate_out = 0.25
rate_point = 0.03
rate_depth = 0.3
rate_gain = 0.45
rate_vector = 0.2


def with_halo(shard, sides, width):
    for axis, dim in sides:
        size, length = (lax.axis_size(axis), shard.shape[dim])
        up = [(i, (i + 1) % size) for i in range(size - 1)]
        down = [(j, i) for i, j in up]
        last = lax.slice_in_dim(shard, length - width, length, axis=dim)
        initial = lax.slice_in_dim(shard, 0, width, axis=dim)
        before = lax.ppermute(last, axis, up)
        after = lax.ppermute(initial, axis, down)
        shard = jnp.concatenate([before, shard, after], axis=dim)
    return shard


def layer_norm(stream, gain_row, shift_row):
    center = stream - jnp.mean(stream, axis=-1, keepdims=True)
    variance = jnp.mean(center * center, axis=-1, keepdims=True)
    inverse = lax.rsqrt(variance + norm_eps)
    normed = center * inverse
    return (normed * gain_row + shift_row, normed, inverse)


def norm_back(upstream, normed, inverse, gain_row):
    scaled = upstream * gain_row
    inner = (
        scaled
        - jnp.mean(scaled, axis=-1, keepdims=True)
        - normed * jnp.mean(scaled * normed, axis=-1, keepdims=True)
    )
    return (
        inverse * inner,
        jnp.sum(upstream * normed, axis=(0, 1)),
        jnp.sum(upstream, axis=(0, 1)),
    )


def tap_mask(paths, taps):
    offsets = jnp.abs(jnp.arange(taps, dtype=jnp.int32) - taps // 2)
    return (offsets[None, :] <= paths[:, None] + 1).astype(jnp.float32)


def grouped(array, group_count):
    return array.reshape((group_count, array.shape[0] // group_count) + array.shape[1:])


def split_heads(array, head_count):
    return array.reshape(array.shape[0], array.shape[1], head_count, array.shape[2] // head_count)


def attend_forward(parts, head_count, score_scale):
    queries, key_rows, value_rows = parts
    query_heads = split_heads(queries, head_count)
    key_heads = split_heads(key_rows, head_count)
    value_heads = split_heads(value_rows, head_count)
    scores = (
        jnp.einsum("pthe,plhe->phtl", query_heads, key_heads, preferred_element_type=jnp.float32)
        * score_scale
    )
    maxima = jnp.max(scores, axis=-1, keepdims=True)
    exponent = jnp.exp(scores - maxima)
    totals = jnp.sum(exponent, axis=-1, keepdims=True)
    attn_probs = (exponent / totals).astype(jnp.bfloat16)
    mixture = jnp.einsum(
        "phtl,plhe->pthe", attn_probs, value_heads, preferred_element_type=jnp.float32
    )
    return (mixture.reshape(queries.shape), (maxima + jnp.log(totals))[..., 0])


def score_grads(query_heads, key_heads, value_heads, grad_heads, log_sums, score_scale):
    scores = (
        jnp.einsum("pthe,plhe->phtl", query_heads, key_heads, preferred_element_type=jnp.float32)
        * score_scale
    )
    attn_probs = jnp.exp(scores - log_sums[..., None])
    grad_probs = jnp.einsum(
        "pthe,plhe->phtl", grad_heads, value_heads, preferred_element_type=jnp.float32
    )
    row_sums = jnp.sum(attn_probs * grad_probs, axis=-1, keepdims=True)
    grad_scores = (attn_probs * (grad_probs - row_sums)).astype(jnp.bfloat16)
    return (attn_probs, grad_scores, row_sums)


def attend_backward(parts, head_count, score_scale):
    queries, key_rows, value_rows, grad_mixed, log_sums = parts
    query_heads = split_heads(queries, head_count)
    key_heads = split_heads(key_rows, head_count)
    value_heads = split_heads(value_rows, head_count)
    grad_heads = split_heads(grad_mixed, head_count)
    attn_probs, grad_scores, row_sums = score_grads(
        query_heads, key_heads, value_heads, grad_heads, log_sums, score_scale
    )
    grad_query = (
        jnp.einsum("phtl,plhe->pthe", grad_scores, key_heads, preferred_element_type=jnp.float32)
        * score_scale
    )
    grad_key = (
        jnp.einsum("phtl,pthe->plhe", grad_scores, query_heads, preferred_element_type=jnp.float32)
        * score_scale
    )
    grad_value = jnp.einsum(
        "phtl,pthe->plhe",
        attn_probs.astype(jnp.bfloat16),
        grad_heads,
        preferred_element_type=jnp.float32,
    )
    return (
        grad_query.reshape(queries.shape),
        grad_key.reshape(key_rows.shape),
        grad_value.reshape(value_rows.shape),
    )


def adam_update(master, first, second, gradient, step_rate):
    first_new = beta_first * first + (1.0 - beta_first) * gradient
    second_new = beta_second * second + (1.0 - beta_second) * gradient * gradient
    first_hat = first_new / (1.0 - beta_first**STEP)
    second_hat = second_new / (1.0 - beta_second**STEP)
    updated = master - step_rate * (
        first_hat / (jnp.sqrt(second_hat) + adam_eps) + weight_decay * master
    )
    return (updated, first_new, second_new, updated.astype(jnp.bfloat16))


def shards(
    inputs,
    masked_positions,
    masked_grads,
    kernel_paths,
    attn_weight,
    out_weight,
    point_weight,
    depth_weight,
    gains,
    shifts,
    first_attn,
    first_out,
    first_point,
    first_depth,
    first_gains,
    first_shifts,
    second_attn,
    second_out,
    second_point,
    second_depth,
    second_gains,
    second_shifts,
):
    seq_count, tok_count, model_width = inputs.shape
    head_count = HEADS
    score_scale = (model_width // head_count) ** (-0.5)
    tap_count = depth_weight.shape[1]
    half_width = tap_count // 2
    per_group = min(seq_count, max(1, 512 // tok_count))
    group_count = seq_count // per_group
    blocks = attn_weight.shape[0]
    gathered = (
        lax.all_gather(attn_weight.astype(jnp.bfloat16), ("seq", "dp"), axis=1, tiled=True),
        lax.all_gather(out_weight.astype(jnp.bfloat16), ("seq", "dp"), axis=1, tiled=True),
        lax.all_gather(point_weight.astype(jnp.bfloat16), ("seq", "dp"), axis=1, tiled=True),
        lax.all_gather(depth_weight.astype(jnp.bfloat16), ("seq", "dp"), axis=2, tiled=True),
        lax.all_gather(gains.astype(jnp.bfloat16), ("seq", "dp"), axis=2, tiled=True),
        lax.all_gather(shifts.astype(jnp.bfloat16), ("seq", "dp"), axis=2, tiled=True),
    )
    attn_all, out_all, point_all = (gathered[0], gathered[1], gathered[2])
    depth_all = gathered[3].astype(jnp.float32)
    gain_all = gathered[4].astype(jnp.float32)
    shift_all = gathered[5].astype(jnp.float32)
    forward_fn = partial(attend_forward, head_count=head_count, score_scale=score_scale)
    backward_fn = partial(attend_backward, head_count=head_count, score_scale=score_scale)
    stream = inputs.astype(jnp.float32)
    saved = []
    for block_num in range(blocks):
        mask_rows = tap_mask(kernel_paths[:, block_num], tap_count)
        tap_weights = depth_all[block_num][None, :, :] * mask_rows[:, :, None]
        flowing_lowered = stream.astype(jnp.bfloat16)
        project_output = jnp.einsum(
            "std,de->ste", flowing_lowered, attn_all[block_num], preferred_element_type=jnp.float32
        )
        queries = (project_output[..., :model_width] + shift_all[block_num, 2]).astype(jnp.bfloat16)
        key_rows = project_output[..., model_width : 2 * model_width].astype(jnp.bfloat16)
        value_rows = project_output[..., 2 * model_width :].astype(jnp.bfloat16)
        key_all, value_all = (
            lax.all_gather(key_rows, "seq", axis=1, tiled=True),
            lax.all_gather(value_rows, "seq", axis=1, tiled=True),
        )
        mixture, log_sums = lax.map(
            forward_fn,
            (
                grouped(queries, group_count),
                grouped(key_all, group_count),
                grouped(value_all, group_count),
            ),
        )
        mixed_lowered = mixture.reshape(seq_count, tok_count, model_width).astype(jnp.bfloat16)
        branch_output = (
            jnp.einsum(
                "std,de->ste", mixed_lowered, out_all[block_num], preferred_element_type=jnp.float32
            )
            + shift_all[block_num, 3]
        )
        middle, normed_one, inverse_one = layer_norm(
            stream + branch_output, gain_all[block_num, 0], shift_all[block_num, 0]
        )
        middle_wide = with_halo(middle.astype(jnp.bfloat16), (("seq", 1),), half_width)
        convolved = jnp.zeros_like(middle)
        for offset in range(tap_count):
            convolved = convolved + tap_weights[:, offset][:, None, :] * middle_wide[
                :, offset : offset + tok_count
            ].astype(jnp.float32)
        convolution_lowered = convolved.astype(jnp.bfloat16)
        pointwise_mixing = (
            jnp.einsum(
                "std,de->ste",
                convolution_lowered,
                point_all[block_num],
                preferred_element_type=jnp.float32,
            )
            + shift_all[block_num, 4]
        )
        stream, normed_two, inverse_two = layer_norm(
            middle + pointwise_mixing, gain_all[block_num, 1], shift_all[block_num, 1]
        )
        held = (key_all, value_all)
        saved.append(
            (
                flowing_lowered,
                queries,
                held,
                (key_rows, value_rows),
                log_sums,
                mixed_lowered,
                normed_one,
                inverse_one,
                middle_wide,
                mask_rows,
                tap_weights,
                convolution_lowered,
                normed_two,
                inverse_two,
            )
        )
    result = stream.astype(jnp.bfloat16)
    token_ids = lax.axis_index("seq") * tok_count + jnp.arange(tok_count, dtype=jnp.int32)
    branch_picks = (masked_positions[:, None, :] == token_ids[None, :, None]).astype(jnp.bfloat16)
    upstream = jnp.einsum(
        "stm,smd->std", branch_picks, masked_grads, preferred_element_type=jnp.float32
    )
    grad_lists = [None] * blocks
    for block_num in reversed(range(blocks)):
        (
            flowing_lowered,
            queries,
            held,
            own_pair,
            log_sums,
            mixed_lowered,
            normed_one,
            inverse_one,
            middle_wide,
            mask_rows,
            tap_weights,
            convolution_lowered,
            normed_two,
            inverse_two,
        ) = saved[block_num]
        grad_two, gain_two, shift_two = norm_back(
            upstream, normed_two, inverse_two, gain_all[block_num, 1]
        )
        grad_point_out = grad_two.astype(jnp.bfloat16)
        bias_point = jnp.sum(grad_point_out.astype(jnp.float32), axis=(0, 1))
        weight_point = jnp.einsum(
            "std,ste->de", convolution_lowered, grad_point_out, preferred_element_type=jnp.float32
        )
        grad_conv = jnp.einsum(
            "ste,de->std", grad_point_out, point_all[block_num], preferred_element_type=jnp.float32
        ).astype(jnp.bfloat16)
        grad_wide = with_halo(grad_conv, (("seq", 1),), half_width)
        grad_float = grad_conv.astype(jnp.float32)
        tap_grads = []
        grad_middle = grad_two
        for offset in range(tap_count):
            tap_grads.append(
                jnp.sum(
                    grad_float * middle_wide[:, offset : offset + tok_count].astype(jnp.float32),
                    axis=1,
                )
            )
            start_row = 2 * half_width - offset
            grad_middle = grad_middle + tap_weights[:, offset][:, None, :] * grad_wide[
                :, start_row : start_row + tok_count
            ].astype(jnp.float32)
        weight_depth = jnp.sum(jnp.stack(tap_grads, axis=1) * mask_rows[:, :, None], axis=0)
        grad_one, gain_one, shift_one = norm_back(
            grad_middle, normed_one, inverse_one, gain_all[block_num, 0]
        )
        grad_branch = grad_one.astype(jnp.bfloat16)
        bias_out = jnp.sum(grad_branch.astype(jnp.float32), axis=(0, 1))
        weight_out = jnp.einsum(
            "std,ste->de", mixed_lowered, grad_branch, preferred_element_type=jnp.float32
        )
        grad_mixed = jnp.einsum(
            "ste,de->std", grad_branch, out_all[block_num], preferred_element_type=jnp.float32
        ).astype(jnp.bfloat16)
        key_all, value_all = held
        grad_query, grad_key_part, grad_value_part = lax.map(
            backward_fn,
            (
                grouped(queries, group_count),
                grouped(key_all, group_count),
                grouped(value_all, group_count),
                grouped(grad_mixed, group_count),
                log_sums,
            ),
        )
        grad_key, grad_value = (
            lax.psum_scatter(
                grad_key_part.reshape(seq_count, -1, model_width).astype(jnp.bfloat16),
                "seq",
                scatter_dimension=1,
                tiled=True,
            ).astype(jnp.float32),
            lax.psum_scatter(
                grad_value_part.reshape(seq_count, -1, model_width).astype(jnp.bfloat16),
                "seq",
                scatter_dimension=1,
                tiled=True,
            ).astype(jnp.float32),
        )
        query_low = grad_query.reshape(seq_count, tok_count, model_width).astype(jnp.bfloat16)
        grad_proj = jnp.concatenate(
            [query_low, grad_key.astype(jnp.bfloat16), grad_value.astype(jnp.bfloat16)], axis=-1
        )
        weight_attn = jnp.einsum(
            "std,ste->de", flowing_lowered, grad_proj, preferred_element_type=jnp.float32
        )
        bias_query = jnp.sum(query_low.astype(jnp.float32), axis=(0, 1))
        upstream = grad_one + jnp.einsum(
            "ste,de->std", grad_proj, attn_all[block_num], preferred_element_type=jnp.float32
        )
        grad_lists[block_num] = (
            weight_attn,
            weight_out,
            weight_point,
            weight_depth,
            jnp.stack([gain_one, gain_two]),
            jnp.stack([shift_one, shift_two, bias_query, bias_out, bias_point]),
        )
    stacked = tuple(
        (
            jnp.stack([grad_lists[block_num][member] for block_num in range(blocks)])
            for member in range(6)
        )
    )
    seq_sums = (
        lax.psum_scatter(
            stacked[0].astype(jnp.bfloat16), "seq", scatter_dimension=1, tiled=True
        ).astype(jnp.float32),
        lax.psum_scatter(
            stacked[1].astype(jnp.bfloat16), "seq", scatter_dimension=1, tiled=True
        ).astype(jnp.float32),
        lax.psum_scatter(
            stacked[2].astype(jnp.bfloat16), "seq", scatter_dimension=1, tiled=True
        ).astype(jnp.float32),
        lax.psum_scatter(
            stacked[3].astype(jnp.bfloat16), "seq", scatter_dimension=2, tiled=True
        ).astype(jnp.float32),
        lax.psum_scatter(
            stacked[4].astype(jnp.bfloat16), "seq", scatter_dimension=2, tiled=True
        ).astype(jnp.float32),
        lax.psum_scatter(
            stacked[5].astype(jnp.bfloat16), "seq", scatter_dimension=2, tiled=True
        ).astype(jnp.float32),
    )
    reduced = (
        lax.psum_scatter(
            seq_sums[0].astype(jnp.bfloat16), "dp", scatter_dimension=1, tiled=True
        ).astype(jnp.float32),
        lax.psum_scatter(
            seq_sums[1].astype(jnp.bfloat16), "dp", scatter_dimension=1, tiled=True
        ).astype(jnp.float32),
        lax.psum_scatter(
            seq_sums[2].astype(jnp.bfloat16), "dp", scatter_dimension=1, tiled=True
        ).astype(jnp.float32),
        lax.psum_scatter(
            seq_sums[3].astype(jnp.bfloat16), "dp", scatter_dimension=2, tiled=True
        ).astype(jnp.float32),
        lax.psum_scatter(
            seq_sums[4].astype(jnp.bfloat16), "dp", scatter_dimension=2, tiled=True
        ).astype(jnp.float32),
        lax.psum_scatter(
            seq_sums[5].astype(jnp.bfloat16), "dp", scatter_dimension=2, tiled=True
        ).astype(jnp.float32),
    )
    masters = (attn_weight, out_weight, point_weight, depth_weight, gains, shifts)
    firsts = (first_attn, first_out, first_point, first_depth, first_gains, first_shifts)
    seconds = (second_attn, second_out, second_point, second_depth, second_gains, second_shifts)
    rates = (rate_attn, rate_out, rate_point, rate_depth, rate_gain, rate_vector)
    updates = [
        adam_update(
            masters[member], firsts[member], seconds[member], reduced[member], rates[member]
        )
        for member in range(6)
    ]
    return (
        (result, upstream)
        + tuple((entry[0] for entry in updates))
        + tuple((entry[1] for entry in updates))
        + tuple((entry[2] for entry in updates))
        + tuple((entry[3] for entry in updates))
    )


def solution(mesh):
    return jax.shard_map(
        shards,
        mesh=mesh,
        in_specs=(
            P("dp", "seq", None),
            P("dp", None),
            P("dp", None, None),
            P("dp", None),
            P(None, ("seq", "dp"), None),
            P(None, ("seq", "dp"), None),
            P(None, ("seq", "dp"), None),
            P(None, None, ("seq", "dp")),
            P(None, None, ("seq", "dp")),
            P(None, None, ("seq", "dp")),
            P(None, ("seq", "dp"), None),
            P(None, ("seq", "dp"), None),
            P(None, ("seq", "dp"), None),
            P(None, None, ("seq", "dp")),
            P(None, None, ("seq", "dp")),
            P(None, None, ("seq", "dp")),
            P(None, ("seq", "dp"), None),
            P(None, ("seq", "dp"), None),
            P(None, ("seq", "dp"), None),
            P(None, None, ("seq", "dp")),
            P(None, None, ("seq", "dp")),
            P(None, None, ("seq", "dp")),
        ),
        out_specs=(
            P("dp", "seq", None),
            P("dp", "seq", None),
            P(None, ("seq", "dp"), None),
            P(None, ("seq", "dp"), None),
            P(None, ("seq", "dp"), None),
            P(None, None, ("seq", "dp")),
            P(None, None, ("seq", "dp")),
            P(None, None, ("seq", "dp")),
            P(None, ("seq", "dp"), None),
            P(None, ("seq", "dp"), None),
            P(None, ("seq", "dp"), None),
            P(None, None, ("seq", "dp")),
            P(None, None, ("seq", "dp")),
            P(None, None, ("seq", "dp")),
            P(None, ("seq", "dp"), None),
            P(None, ("seq", "dp"), None),
            P(None, ("seq", "dp"), None),
            P(None, None, ("seq", "dp")),
            P(None, None, ("seq", "dp")),
            P(None, None, ("seq", "dp")),
            P(None, ("seq", "dp"), None),
            P(None, ("seq", "dp"), None),
            P(None, ("seq", "dp"), None),
            P(None, None, ("seq", "dp")),
            P(None, None, ("seq", "dp")),
            P(None, None, ("seq", "dp")),
        ),
        check_vma=False,
    )
```

profile of v0, /device:TPU:0, one launch (start us, length us, event | category | flops | bytes accessed | tf_op | source)
XLA Modules:
  0.0 1085.5 jit_solution(15966787723338218980)
XLA Ops:
  9.2 78.1 %all-gather.8.cloned.1.call-done = bf16[2,768,2304]{2,1,0:T(8,128)(2,1)} async-done(((bf16[2,24,2304]{2,1,0:T(8,128)(2,1)}), bf16[2,768,2304]{2,1,0:T(8,128)(2,1)}) %all-gather.8.cloned.1.call-update) | async-done | bytes 7077904 | tf_op jit(solution)/shard_map/all_gather | solution.py:180
  96.4 41.3 %all_gather.35 = bf16[2,2,768]{1,0,2:T(2,128)(2,1)S(1)} all-gather(bf16[2,2,24]{1,0,2:T(2,128)(2,1)S(1)} %copy.236), channel_id=1, replica_groups=mesh['seq'=4,'dp'=8] {'seq','dp'}, dimensions={2}, use_global_device_ids=true | all-gather | bytes 6336 | tf_op jit(solution)/shard_map/all_gather | solution.py:184
  137.7 38.7 %all_gather.32 = bf16[2,5,768]{1,0,2:T(2,128)(2,1)S(1)} all-gather(bf16[2,5,24]{1,0,2:T(2,128)(2,1)S(1)} %copy.232), channel_id=1, replica_groups=mesh['seq'=4,'dp'=8] {'seq','dp'}, dimensions={2}, use_global_device_ids=true | all-gather | bytes 15840 | tf_op jit(solution)/shard_map/all_gather | solution.py:185
  176.4 39.9 %all_gather.36 = bf16[2,7,768]{1,0,2:T(2,128)(2,1)S(1)} all-gather(bf16[2,7,24]{1,0,2:T(2,128)(2,1)S(1)} %copy.237), channel_id=1, replica_groups=mesh['seq'=4,'dp'=8] {'seq','dp'}, dimensions={2}, use_global_device_ids=true | all-gather | bytes 22176 | tf_op jit(solution)/shard_map/all_gather | solution.py:183
  217.5 26.7 %slice_reduce_fusion = (f32[768]{0:T(1024)}, f32[768]{0:T(1024)}, f32[768]{0:T(1024)}, f32[768]{0:T(1024)}, f32[768]{0:T(1024)}, /*index=5*/f32[768]{0:T(1024)S(...) fusion(f32[2,5,768]{1,0,2:T(2,128)S(1)} %convert_element_type.389), kind=kLoop, calls=%fused_computation.220 | loop fusion | bytes 61440 | tf_op jit(solution)/shard_map/slice | solution.py:244
  244.5 9.7 slice_reduce_fusion.1
  286.9 6.9 all-gather.16.cloned.1.call-done
  296.2 5.5 fusion.156
  305.4 33.9 %all-gather.20.cloned.1.call-done = bf16[3,512,768]{2,1,0:T(8,128)(2,1)} async-done(((bf16[3,128,768]{2,1,0:T(8,128)(2,1)}), bf16[3,512,768]{2,1,0:T(8,128)(2,1)}) %all-gather.20.cloned.1.call-update) | async-done | bytes 2359312 | tf_op jit(solution)/shard_map/all_gather | solution.py:206
  352.8 25.9 %all-gather.18.cloned.1.call-done = bf16[3,512,768]{2,1,0:T(8,128)(2,1)} async-done(((bf16[3,128,768]{2,1,0:T(8,128)(2,1)}), bf16[3,512,768]{2,1,0:T(8,128)(2,1)}) %all-gather.18.cloned.1.call-update) | async-done | bytes 2359312 | tf_op jit(solution)/shard_map/all_gather | solution.py:207
  383.0 6.0 fusion.36
  422.2 7.2 fusion.20
  433.7 6.1 multiply_reduce_fusion.1
  439.8 5.9 multiply_convert_fusion.1
  459.3 15.0 %reduce-scatter.27.cloned.1.call-done = bf16[3,128,768]{2,1,0:T(8,128)(2,1)} async-done(((bf16[3,512,768]{2,1,0:T(8,128)(2,1)}), bf16[3,128,768]{2,1,0:T(8,128)(2,1)}) %reduce-scatter.27.cloned.1.call-update) | async-done | bytes 589840 | tf_op jit(solution)/shard_map/reduce_scatter | solution.py:345
  474.4 40.5 %reduce-scatter.25.cloned.1.call-done = bf16[3,128,768]{2,1,0:T(8,128)(2,1)} async-done(((bf16[3,512,768]{2,1,0:T(8,128)(2,1)}), bf16[3,128,768]{2,1,0:T(8,128)(2,1)}) %reduce-scatter.25.cloned.1.call-update) | async-done | bytes 589840 | tf_op jit(solution)/shard_map/reduce_scatter | solution.py:339
  538.2 7.3 fusion.23
  549.8 6.1 multiply_reduce_fusion
  555.9 5.6 multiply_convert_fusion
  583.9 5.5 fusion.15
  595.5 34.9 %reduce-scatter.29.cloned.1.call-done = bf16[3,128,768]{2,1,0:T(8,128)(2,1)} async-done(((bf16[3,512,768]{2,1,0:T(8,128)(2,1)}), bf16[3,128,768]{2,1,0:T(8,128)(2,1)}) %reduce-scatter.29.cloned.1.call-update) | async-done | bytes 589840 | tf_op jit(solution)/shard_map/reduce_scatter | solution.py:339
  637.3 18.5 %copy.254 = bf16[2,768,2304]{2,0,1:T(2,128)(2,1)} copy(bf16[2,768,2304]{1,2,0:T(8,128)(2,1)} %pad_maximum_fusion) | data formatting | bytes 14155776 | tf_op jit(solution)/shard_map/stack | solution.py:373
  655.9 14.8 %reduce-scatter.35.cloned.1.call-done = bf16[2,192,768]{2,1,0:T(8,128)(2,1)} async-done(((bf16[2,768,768]{2,1,0:T(8,128)(2,1)}), bf16[2,192,768]{2,1,0:T(8,128)(2,1)}) %reduce-scatter.35.cloned.1.call-update) | async-done | bytes 589840 | tf_op jit(solution)/shard_map/reduce_scatter | solution.py:384
  673.6 37.6 %reduce-scatter.33.cloned.1.call-done = bf16[2,192,768]{2,1,0:T(8,128)(2,1)} async-done(((bf16[2,768,768]{2,1,0:T(8,128)(2,1)}), bf16[2,192,768]{2,1,0:T(8,128)(2,1)}) %reduce-scatter.33.cloned.1.call-update) | async-done | bytes 589840 | tf_op jit(solution)/shard_map/reduce_scatter | solution.py:381
  716.4 22.0 %reduce-scatter.43.cloned.1.call-done = bf16[192,4]{1,0:T(8,128)(2,1)} async-done(((bf16[768,4]{1,0:T(8,128)(2,1)}), bf16[192,4]{1,0:T(8,128)(2,1)}) %reduce-scatter.43.cloned.1.call-update) | async-done | bytes 1552
  739.4 26.2 %reduce-scatter.41.cloned.1.call-done = bf16[192,14]{1,0:T(8,128)(2,1)} async-done(((bf16[768,14]{1,0:T(8,128)(2,1)}), bf16[192,14]{1,0:T(8,128)(2,1)}) %reduce-scatter.41.cloned.1.call-update) | async-done | bytes 5392
  766.6 26.2 %reduce-scatter.45.cloned.1.call-done = bf16[192,10]{1,0:T(8,128)(2,1)} async-done(((bf16[768,10]{1,0:T(8,128)(2,1)}), bf16[192,10]{1,0:T(8,128)(2,1)}) %reduce-scatter.45.cloned.1.call-update) | async-done | bytes 3856
  793.8 28.1 %all-reduce.5 = (bf16[2,7,192]{2,1,0:T(8,128)(2,1)S(1)}, bf16[2,2,192]{2,1,0:T(2,128)(2,1)S(1)}, bf16[2,5,192]{2,1,0:T(8,128)(2,1)S(1)}) all-reduce(bf16[2,7,192]{2,1,0:T(8,128)(2,1)S(1)} %copy.287, bf16[2,2,192]{2,1,0:T(2,128)(2,1)S(1)} %copy.291, bf16[2,5,192]{2,1,0:T(8,128)(2,1)S(1)} %copy.295), channel_id=13, replica_groups=mesh['seq'=4,'dp'=8] {'dp'}, use_global_device_ids=true, to_apply=%region_49.50.clone | all-reduce | flops 5376 | bytes 21504
  827.5 119.9 %all-reduce.9.cloned.1.call-done = bf16[2,768,2304]{2,0,1:T(2,128)(2,1)} async-done(((bf16[2,768,2304]{2,0,1:T(2,128)(2,1)}), bf16[2,768,2304]{2,0,1:T(2,128)(2,1)}) %all-reduce.9.cloned.1.call-update) | async-done | bytes 7077904
  957.8 22.9 %reduce-scatter.39.cloned.1.call-done = bf16[24,1536]{1,0:T(8,128)(2,1)} async-done(((bf16[192,1536]{1,0:T(8,128)(2,1)}), bf16[24,1536]{1,0:T(8,128)(2,1)}) %reduce-scatter.39.cloned.1.call-update) | async-done | bytes 73744
  983.6 28.8 %reduce-scatter.37.cloned.1.call-done = bf16[24,1536]{1,0:T(8,128)(2,1)} async-done(((bf16[192,1536]{1,0:T(8,128)(2,1)}), bf16[24,1536]{1,0:T(8,128)(2,1)}) %reduce-scatter.37.cloned.1.call-update) | async-done | bytes 73744
  1014.1 61.5 %all-reduce.11.cloned.1.call-done = bf16[2,192,2304]{2,0,1:T(2,128)(2,1)} async-done(((bf16[2,192,2304]{2,0,1:T(2,128)(2,1)}), bf16[2,192,2304]{2,0,1:T(2,128)(2,1)}) %all-reduce.11.cloned.1.call-update) | async-done | bytes 1769488
  (425 shorter events, 214.8 us)
Async XLA Ops:
  7.2 395.0 %copy-start = (bf16[3,76,768]{2,1,0:T(8,128)(2,1)S(1)}, bf16[3,76,768]{2,1,0:T(8,128)(2,1)}, u32[]{:S(2)}) copy-start(bf16[3,76,768]{2,1,0:T(8,128)(2,1)} %param.24) | copy-start | bytes 1050628
  7.2 80.0 %all-gather.8.cloned.1.call-start = ((), (), s32[]{:S(2)}) async-start(), calls=%async_computation.11 | async-start | bytes 7299072 | tf_op jit(solution)/shard_map/all_gather | solution.py:180
  9.1 247.6 %all-gather.12.cloned.1.call-start = ((), (), s32[]{:S(2)}) async-start(), calls=%async_computation.13 | async-start | bytes 2949120 | tf_op jit(solution)/shard_map/all_gather | solution.py:206
  93.7 166.0 %all-gather.10.cloned.1.call-start = ((), (), s32[]{:S(2)}) async-start(), calls=%async_computation.12 | async-start | bytes 2949120 | tf_op jit(solution)/shard_map/all_gather | solution.py:207
  94.5 179.8 %all-gather.14.cloned.1.call-start = ((), (), s32[]{:S(2)}) async-start(), calls=%async_computation.14 | async-start | bytes 2433024 | tf_op jit(solution)/shard_map/all_gather | solution.py:181
  95.2 198.6 %all-gather.16.cloned.1.call-start = ((), (), s32[]{:S(2)}) async-start(), calls=%async_computation.15 | async-start | bytes 2433024 | tf_op jit(solution)/shard_map/all_gather | solution.py:182
  96.0 243.3 %all-gather.20.cloned.1.call-start = ((), (), s32[]{:S(2)}) async-start(), calls=%async_computation.17 | async-start | bytes 2949120 | tf_op jit(solution)/shard_map/all_gather | solution.py:206
  277.1 2.9 collective-permute-start
  278.4 6.8 collective-permute-start.1
  302.8 75.9 %all-gather.18.cloned.1.call-start = ((), (), s32[]{:S(2)}) async-start(), calls=%async_computation.16 | async-start | bytes 2949120 | tf_op jit(solution)/shard_map/all_gather | solution.py:207
  303.5 170.8 %reduce-scatter.27.cloned.1.call-start = ((), (), s32[]{:S(2)}) async-start(), calls=%async_computation.19 | async-start | bytes 2949120 | tf_op jit(solution)/shard_map/reduce_scatter | solution.py:345
  390.9 5.2 collective-permute-start.2
  394.4 5.7 collective-permute-start.3
  407.3 6.2 collective-permute-start.4
  408.6 6.3 collective-permute-start.5
  433.6 81.2 %reduce-scatter.25.cloned.1.call-start = ((), (), s32[]{:S(2)}) async-start(), calls=%async_computation.18 | async-start | bytes 2949120 | tf_op jit(solution)/shard_map/reduce_scatter | solution.py:339
  453.1 142.4 %reduce-scatter.31.cloned.1.call-start = ((), (), s32[]{:S(2)}) async-start(), calls=%async_computation.21 | async-start | bytes 2949120 | tf_op jit(solution)/shard_map/reduce_scatter | solution.py:345
  523.1 5.9 collective-permute-start.6
  524.4 6.0 collective-permute-start.7
  549.7 80.6 %reduce-scatter.29.cloned.1.call-start = ((), (), s32[]{:S(2)}) async-start(), calls=%async_computation.20 | async-start | bytes 2949120 | tf_op jit(solution)/shard_map/reduce_scatter | solution.py:339
  568.7 102.0 %reduce-scatter.35.cloned.1.call-start = ((), (), s32[]{:S(2)}) async-start(), calls=%async_computation.23 | async-start | bytes 2949120 | tf_op jit(solution)/shard_map/reduce_scatter | solution.py:384
  574.2 136.9 %reduce-scatter.33.cloned.1.call-start = ((), (), s32[]{:S(2)}) async-start(), calls=%async_computation.22 | async-start | bytes 2949120 | tf_op jit(solution)/shard_map/reduce_scatter | solution.py:381
  579.7 158.7 %reduce-scatter.43.cloned.1.call-start = ((), (), s32[]{:S(2)}) async-start(), calls=%async_computation.27 | async-start | bytes 245760
  582.4 183.2 %reduce-scatter.41.cloned.1.call-start = ((), (), s32[]{:S(2)}) async-start(), calls=%async_computation.26 | async-start | bytes 245760
  583.9 208.9 %reduce-scatter.45.cloned.1.call-start = ((), (), s32[]{:S(2)}) async-start(), calls=%async_computation.28 | async-start | bytes 245760
  595.4 352.0 %all-reduce.9.cloned.1.call-start = ((), (), s32[]{:S(2)}) async-start(), calls=%async_computation.29 | async-start | bytes 14155776
  655.9 324.9 %reduce-scatter.39.cloned.1.call-start = ((), (), s32[]{:S(2)}) async-start(), calls=%async_computation.25 | async-start | bytes 663552
  673.3 339.1 %reduce-scatter.37.cloned.1.call-start = ((), (), s32[]{:S(2)}) async-start(), calls=%async_computation.24 | async-start | bytes 663552
  713.0 113.9 %copy-start.78 = (f32[2,2,24]{2,1,0:T(2,128)S(1)}, f32[2,2,24]{2,1,0:T(2,128)}, u32[]{:S(2)}) copy-start(f32[2,2,24]{2,1,0:T(2,128)} %param.30) | copy-start | bytes 1156
  713.0 113.9 %copy-start.87 = (f32[2,2,24]{2,1,0:T(2,128)S(1)}, f32[2,2,24]{2,1,0:T(2,128)}, u32[]{:S(2)}) copy-start(f32[2,2,24]{2,1,0:T(2,128)} %param.36) | copy-start | bytes 1156
  713.0 113.9 %copy-start.88 = (f32[2,2,24]{2,1,0:T(2,128)S(1)}, f32[2,2,24]{2,1,0:T(2,128)}, u32[]{:S(2)}) copy-start(f32[2,2,24]{2,1,0:T(2,128)} %param.42) | copy-start | bytes 1156
  713.9 361.8 %all-reduce.11.cloned.1.call-start = ((), (), s32[]{:S(2)}) async-start(), calls=%async_computation.30 | async-start | bytes 3538944
  (91 other events, 1709.6 us)
Sparse Core Ops, SparseCore 0:
  11.8 75.3 all-gather.7
  93.8 37.1 all-gather.11
  133.5 38.3 all-gather.9
  175.5 57.8 all-gather.13
  237.0 56.7 all-gather.15
  302.9 36.3 all-gather.19
  341.1 37.4 all-gather.17
  433.7 40.5 reduce-scatter.26
  477.4 37.3 reduce-scatter.24
  549.9 39.9 reduce-scatter.30
  592.9 37.3 reduce-scatter.28
  633.3 37.3 reduce-scatter.34
  673.7 37.3 reduce-scatter.32
  714.4 23.9 reduce-scatter.42
  741.6 23.9 reduce-scatter.40
  768.8 23.9 reduce-scatter.44
  796.0 151.3 all-reduce.8
  949.6 31.1 reduce-scatter.38
  983.0 29.2 reduce-scatter.36
  1014.6 61.0 all-reduce.10
where the time goes:
time: 1100 us; the launch traced here: 1090 us
  waiting for transfers between devices  609 us (55%)
  blocking collectives  148 us (13%)
  local copies, waits for them, and re-layouts  138 us (13%)
  matrix products  106 us (10%)
  other arithmetic  45.6 us (4%)
  starting transfers between devices  21.3 us (2%)
  between operations  17.7 us (2%)
    unnamed x27, waiting for transfers between devices  309 us
    all_gather x1, waiting for transfers between devices, shards(): lax.all_gather(attn_weight.astype(jnp.bfloat16), ('seq', 'dp'), axis=1, t...  78.1 us
    reduce_scatter x2, waiting for transfers between devices, shards(): lax.psum_scatter(grad_key_part.reshape(seq_count, -1, model_width).astype...  75.3 us
    all_gather x1, blocking collectives, shards(): lax.all_gather(gains.astype(jnp.bfloat16), ('seq', 'dp'), axis=2, tiled=T...  41.3 us
    unnamed x232, local copies, waits for them, and re-layouts  40.3 us
    all_gather x1, blocking collectives, shards(): lax.all_gather(depth_weight.astype(jnp.bfloat16), ('seq', 'dp'), axis=2,...  39.9 us
    all_gather x1, blocking collectives, shards(): lax.all_gather(shifts.astype(jnp.bfloat16), ('seq', 'dp'), axis=2, tiled=...  38.7 us
    reduce_scatter x1, waiting for transfers between devices, shards(): lax.psum_scatter(stacked[1].astype(jnp.bfloat16), 'seq', scatter_dimensio...  37.6 us
  transfers between devices with their start and end apart: 28, of which 21 were waited for; matrix products, arithmetic and copies ran while one was open for 18% of the time, Pallas kernels for 0%

commit v1 on v0

v1 whole, which is shorter than its diff:
```python
from functools import partial

import jax
import jax.numpy as jnp
from jax import lax
from jax.experimental import pallas as pl
from jax.experimental.pallas import tpu as pltpu
from jax.sharding import PartitionSpec as P

HEADS = 12
STEP = 10

norm_eps = 1e-05
beta_first = 0.5
beta_second = 0.5
adam_eps = 1e-08
weight_decay = 0.01
rate_attn = 0.03
rate_out = 0.25
rate_point = 0.03
rate_depth = 0.3
rate_gain = 0.45
rate_vector = 0.2

f32 = jnp.float32
bf16 = jnp.bfloat16
AXES = ("seq", "dp")
VMEM_BYTES = 56 * 2**20
GROUP = 256
ROWS = 64
PAD = 8

GAIN = 7
SHIFT = 9
SMALL = 14


def dot_nn(a, b):
    return lax.dot_general(a, b, (((1,), (0,)), ((), ())), preferred_element_type=f32)


def dot_nt(a, b):
    return lax.dot_general(a, b, (((1,), (1,)), ((), ())), preferred_element_type=f32)


def dot_tn(a, b):
    return lax.dot_general(a, b, (((0,), (0,)), ((), ())), preferred_element_type=f32)


def vmem_spec():
    return pl.BlockSpec(memory_space=pltpu.VMEM)


def smem_spec():
    return pl.BlockSpec(memory_space=pltpu.SMEM)


def any_spec():
    return pl.BlockSpec(memory_space=pl.ANY)


def call(body, outs, in_specs, scratch, cost, name):
    return pl.pallas_call(
        body,
        out_shape=outs,
        in_specs=in_specs,
        out_specs=jax.tree.map(lambda _: vmem_spec(), outs),
        scratch_shapes=scratch,
        compiler_params=pltpu.CompilerParams(vmem_limit_bytes=VMEM_BYTES),
        cost_estimate=pl.CostEstimate(flops=cost, bytes_accessed=4 * 2**20, transcendentals=0),
        name=name,
    )


def row_loop(total, body, rows=ROWS):
    def step(i, carry):
        body(pl.multiple_of(i * rows, rows))
        return carry

    lax.fori_loop(0, total // rows, step, 0)


def weight_copies(meta, pieces, dest, sem, columns=None):
    s, z, c = meta[0], meta[1], meta[2]
    seqs = len(pieces) // 2
    copies = []
    for j in range(2):
        for k in range(seqs):
            piece = pieces[j * seqs + k]
            subs, rows, width = piece.shape
            first, half = columns if columns else (0, width)
            for m in range(subs):
                row = pl.multiple_of(((k ^ s) * subs + (m ^ z)) * rows, rows)
                col = pl.multiple_of((j ^ c) * half, 128)
                copies.append(
                    pltpu.make_async_copy(
                        piece.at[m, :, pl.ds(first, half)] if columns else piece.at[m],
                        dest.at[pl.ds(row, rows), pl.ds(col, half)],
                        sem,
                    )
                )
    return copies


def head_masks(scale):
    lane = lax.broadcasted_iota(jnp.int32, (1, GROUP), 1) // (GROUP // 4)
    return [jnp.where(lane == h, f32(scale), f32(0)).astype(bf16) for h in range(4)]


def attend_kernel(x_parts, seqs, scale, meta, small, *refs):
    x_refs, pieces = refs[:x_parts], refs[x_parts : x_parts + 2 * seqs]
    x_out, xt_out, qkv, o_out, ot_out, lse_out, weight, x_sem, w_sem = refs[x_parts + 2 * seqs :]
    copies = weight_copies(meta, pieces, weight, w_sem)
    for copy in copies:
        copy.start()
    if x_parts > 1:
        part_rows = x_refs[0].shape[0]
        x_copies = [
            pltpu.make_async_copy(
                x_refs[k],
                x_out.at[pl.ds(pl.multiple_of((k ^ meta[0]) * part_rows, part_rows), part_rows)],
                x_sem,
            )
            for k in range(x_parts)
        ]
        for copy in x_copies:
            copy.start()
        for copy in x_copies:
            copy.wait()
    else:
        x_out[...] = x_refs[0][...]
    xt_out[...] = x_out[...].T
    for copy in copies:
        copy.wait()
    tokens, width = x_out.shape
    scaled, plain = head_masks(scale), head_masks(1.0)
    lane = lax.broadcasted_iota(jnp.int32, (tokens, 128), 1)
    sums = jnp.zeros((tokens, 128), f32)
    for g in range(width // GROUP):
        cols = slice(g * GROUP, (g + 1) * GROUP)
        cols_k = slice(width + g * GROUP, width + (g + 1) * GROUP)
        cols_v = slice(2 * width + g * GROUP, 2 * width + (g + 1) * GROUP)
        bias = small[SHIFT + 2 : SHIFT + 3, cols]
        qkv[:, cols] = (dot_nn(x_out[...], weight[:, cols]) + bias).astype(bf16)
        qkv[:, cols_k] = dot_nn(x_out[...], weight[:, cols_k]).astype(bf16)
        qkv[:, cols_v] = dot_nn(x_out[...], weight[:, cols_v]).astype(bf16)
        mixed = jnp.zeros((tokens, GROUP), f32)
        for h in range(4):
            scores = dot_nt(qkv[:, cols] * scaled[h], qkv[:, cols_k])
            top = jnp.max(scores, axis=-1, keepdims=True)
            weights = jnp.exp(scores - top)
            total = jnp.sum(weights, axis=-1, keepdims=True)
            part = dot_nn(weights.astype(bf16), qkv[:, cols_v] * plain[h])
            mixed = mixed + part * (1.0 / total)
            sums = jnp.where(lane == g * 4 + h, top + jnp.log(total), sums)
        o_out[:, cols] = mixed.astype(bf16)
    ot_out[...] = o_out[...].T
    lse_out[...] = sums.T


def tap_rows(meta, small, block, taps):
    path = meta[3 + block]
    half = taps // 2
    return [
        small[j : j + 1, :] * jnp.where(path + 1 >= abs(j - half), f32(1), f32(0))
        for j in range(taps)
    ]


def norm_rows(r, gain, shift):
    center = r - jnp.mean(r, axis=-1, keepdims=True)
    inverse = lax.rsqrt(jnp.mean(center * center, axis=-1, keepdims=True) + norm_eps)
    normed = center * inverse
    return normed * gain + shift, normed, inverse


def mix_kernel(block, seqs, taps, relative, meta, small, x_ref, o_ref, *refs):
    pieces = refs[: 2 * seqs]
    y_out, y_low, xh1, inv1, xh2, inv2, hct, w_out, w_point, acc, y1, zpad, hc, sem = refs[2 * seqs :]
    tokens, width = o_ref.shape
    half = width // 2
    copies = weight_copies(meta, pieces, w_out, sem, (0, half)) + weight_copies(
        meta, pieces, w_point, sem, (half, half)
    )
    for copy in copies:
        copy.start()
    for copy in copies:
        copy.wait()
    zpad[0:PAD, :] = jnp.zeros((PAD, width), f32)
    zpad[tokens + PAD :, :] = jnp.zeros((PAD, width), f32)
    for n in range(width // GROUP):
        cols = slice(n * GROUP, (n + 1) * GROUP)
        acc[:, cols] = dot_nn(o_ref[...], w_out[:, cols])

    def first_norm(row):
        rows = pl.ds(row, ROWS)
        stream = x_ref[rows, :].astype(f32) + (acc[rows, :] + small[SHIFT + 3 : SHIFT + 4, :])
        out, normed, inverse = norm_rows(
            stream, small[GAIN : GAIN + 1, :], small[SHIFT : SHIFT + 1, :]
        )
        y1[rows, :] = out
        xh1[rows, :] = normed
        inv1[rows, :] = inverse
        zpad[pl.ds(row + PAD, ROWS), :] = out.astype(bf16).astype(f32)

    row_loop(tokens, first_norm)
    weights = tap_rows(meta, small, block, taps)
    reach = taps // 2

    def convolve(row):
        window = zpad[pl.ds(row, ROWS + 2 * PAD), :]
        total = jnp.zeros((ROWS, width), f32)
        for j in range(taps):
            start = PAD - reach + j
            total = total + weights[j] * window[start : start + ROWS]
        hc[pl.ds(row, ROWS), :] = total.astype(bf16)

    row_loop(tokens, convolve)
    for n in range(width // GROUP):
        cols = slice(n * GROUP, (n + 1) * GROUP)
        acc[:, cols] = dot_nn(hc[...], w_point[:, cols])

    def second_norm(row):
        rows = pl.ds(row, ROWS)
        stream = y1[rows, :] + (acc[rows, :] + small[SHIFT + 4 : SHIFT + 5, :])
        out, normed, inverse = norm_rows(
            stream, small[GAIN + 1 : GAIN + 2, :], small[SHIFT + 1 : SHIFT + 2, :]
        )
        xh2[rows, :] = normed
        inv2[rows, :] = inverse
        if not relative:
            y_out[rows, :] = out
            y_low[rows, :] = out.astype(bf16)
        else:
            part = tokens // relative
            y_low[(row // part) ^ meta[0], pl.ds(row % part, ROWS), :] = out.astype(bf16)

    row_loop(tokens, second_norm)
    hct[...] = hc[...].T


def norm_rows_back(upstream, normed, inverse, gain):
    scaled = upstream * gain
    inner = (
        scaled
        - jnp.mean(scaled, axis=-1, keepdims=True)
        - normed * jnp.mean(scaled * normed, axis=-1, keepdims=True)
    )
    return inverse * inner


def column_sum(a):
    return jnp.sum(a, axis=0, keepdims=True)


def store_parts(out, columns, value, meta):
    seqs, subs, rows, _ = out.shape
    for k in range(seqs):
        for m in range(subs):
            start = (k * subs + m) * rows
            out[k ^ meta[0], m ^ meta[1], :, columns] = value[start : start + rows].astype(bf16)


def unmix_kernel(block, seqs, taps, last, meta, small, *refs):
    if last:
        places, grads = refs[:2]
        refs = refs[2:]
    else:
        dy_ref = refs[0]
        refs = refs[1:]
    xh2, inv2, xh1, inv1, hct, ot = refs[:6]
    pieces = refs[6 : 6 + 2 * seqs]
    dr1, do_out, keep, send, sums, w_out, w_point, dr2, du, dpad, zpad, sem = refs[6 + 2 * seqs :]
    tokens, width = dr1.shape
    half = width // 2
    copies = weight_copies(meta, pieces, w_point, sem, (half, half)) + weight_copies(
        meta, pieces, w_out, sem, (0, half)
    )
    for copy in copies:
        copy.start()
    sums[...] = jnp.zeros_like(sums)
    if last:
        picked = places.shape[1]
        token = lax.broadcasted_iota(jnp.int32, (tokens, picked), 0)
        live = jnp.where(meta[5] > 0, f32(1), f32(0))
        picks = jnp.where(token == places[...], live, f32(0)).astype(bf16)
        dr2[...] = dot_nn(picks, grads[...])
    for pad in (dpad, zpad):
        pad[0:PAD, :] = jnp.zeros((PAD, width), f32)
        pad[tokens + PAD :, :] = jnp.zeros((PAD, width), f32)

    def second_norm(row):
        rows = pl.ds(row, ROWS)
        dy = dr2[rows, :] if last else dy_ref[rows, :]
        normed = xh2[rows, :]
        back = norm_rows_back(dy, normed, inv2[rows, :], small[GAIN + 1 : GAIN + 2, :])
        low = back.astype(bf16)
        dr2[rows, :] = back
        du[rows, :] = low
        sums[GAIN + 1 : GAIN + 2, :] += column_sum(dy * normed)
        sums[SHIFT + 1 : SHIFT + 2, :] += column_sum(dy)
        sums[SHIFT + 4 : SHIFT + 5, :] += column_sum(low.astype(f32))
        z = xh1[rows, :] * small[GAIN : GAIN + 1, :] + small[SHIFT : SHIFT + 1, :]
        zpad[pl.ds(row + PAD, ROWS), :] = z.astype(bf16).astype(f32)

    row_loop(tokens, second_norm)
    for copy in copies:
        copy.wait()
    c = meta[2]
    mine = pl.ds(pl.multiple_of(c * half, 128), half)
    other = pl.ds(pl.multiple_of((1 - c) * half, 128), half)
    point_cols, out_cols = slice(half, width), slice(0, half)
    for n in range(width // GROUP):
        cols = slice(n * GROUP, (n + 1) * GROUP)
        back = dot_nt(du[...], w_point[cols, :])
        dpad[PAD : PAD + tokens, cols] = back.astype(bf16).astype(f32)
    store_parts(send, point_cols, dot_nn(hct[...], du[:, other]), meta)
    store_parts(keep, point_cols, dot_nn(hct[...], du[:, mine]), meta)
    weights = tap_rows(meta, small, block, taps)
    path = meta[3 + block]
    reach = taps // 2

    def unconvolve(row):
        rows = pl.ds(row, ROWS)
        window = dpad[pl.ds(row, ROWS + 2 * PAD), :]
        z_window = zpad[pl.ds(row, ROWS + 2 * PAD), :]
        here = window[PAD : PAD + ROWS]
        total = dr2[rows, :]
        for j in range(taps):
            start = PAD + reach - j
            total = total + weights[j] * window[start : start + ROWS]
            z_start = PAD - reach + j
            sums[j : j + 1, :] += column_sum(here * z_window[z_start : z_start + ROWS])
        normed = xh1[rows, :]
        back = norm_rows_back(total, normed, inv1[rows, :], small[GAIN : GAIN + 1, :])
        low = back.astype(bf16)
        dr1[rows, :] = back
        du[rows, :] = low
        sums[GAIN : GAIN + 1, :] += column_sum(total * normed)
        sums[SHIFT : SHIFT + 1, :] += column_sum(total)
        sums[SHIFT + 3 : SHIFT + 4, :] += column_sum(low.astype(f32))

    row_loop(tokens, unconvolve)
    for j in range(taps):
        used = jnp.where(path + 1 >= abs(j - reach), f32(1), f32(0))
        sums[j : j + 1, :] = sums[j : j + 1, :] * used
    for n in range(width // GROUP):
        cols = slice(n * GROUP, (n + 1) * GROUP)
        do_out[:, cols] = dot_nt(du[...], w_out[cols, :]).astype(bf16)
    store_parts(send, out_cols, dot_nn(ot[...], du[:, other]), meta)
    store_parts(keep, out_cols, dot_nn(ot[...], du[:, mine]), meta)


def unattend_kernel(scale, meta, qkv, do_ref, lse, xt, dqkv, keep, send, bias):
    tokens, width = do_ref.shape
    scaled, plain = head_masks(scale), head_masks(1.0)
    for g in range(width // GROUP):
        cols = slice(g * GROUP, (g + 1) * GROUP)
        cols_k = slice(width + g * GROUP, width + (g + 1) * GROUP)
        cols_v = slice(2 * width + g * GROUP, 2 * width + (g + 1) * GROUP)
        dq = jnp.zeros((tokens, GROUP), f32)
        dk = jnp.zeros((tokens, GROUP), f32)
        dv = jnp.zeros((tokens, GROUP), f32)
        for h in range(4):
            q = qkv[:, cols] * scaled[h]
            do = do_ref[:, cols] * plain[h]
            scores = dot_nt(qkv[:, cols_k], q)
            probs = jnp.exp(scores - lse[g * 4 + h : g * 4 + h + 1, :])
            dp = dot_nt(qkv[:, cols_v], do)
            weighted = probs * dp
            ds = (weighted - probs * column_sum(weighted)).astype(bf16)
            dv = dv + dot_nn(probs.astype(bf16), do)
            dk = dk + dot_nn(ds, q)
            dq = dq + dot_tn(ds, qkv[:, cols_k] * scaled[h])
        low = dq.astype(bf16)
        dqkv[:, cols] = low
        bias[:, cols] = column_sum(low.astype(f32))
        dqkv[:, cols_k] = dk.astype(bf16)
        dqkv[:, cols_v] = dv.astype(bf16)
    half = 3 * width // 2
    part = half // 3
    for out, j in ((send, 1 - meta[2]), (keep, meta[2])):
        for t in range(3):
            cols = pl.ds(pl.multiple_of(j * half + t * part, 128), part)
            store_parts(out, slice(t * part, (t + 1) * part), dot_nn(xt[...], dqkv[:, cols]), meta)


def unproject_kernel(seqs, relative, meta, dqkv, dr1, *refs):
    pieces = refs[: 2 * seqs]
    out, weight, sem = refs[2 * seqs :]
    copies = weight_copies(meta, pieces, weight, sem)
    for copy in copies:
        copy.start()
    for copy in copies:
        copy.wait()
    tokens, width = dr1.shape
    for n in range(width // GROUP):
        cols = slice(n * GROUP, (n + 1) * GROUP)
        value = dr1[:, cols] + dot_nt(dqkv[...], weight[cols, :])
        if not relative:
            out[:, cols] = value
        else:
            part = tokens // relative
            for t in range(relative):
                out[t ^ meta[0], :, cols] = value[t * part : (t + 1) * part].astype(bf16)


def adam_update(master, first, second, gradient, step_rate):
    first_new = beta_first * first + (1.0 - beta_first) * gradient
    second_new = beta_second * second + (1.0 - beta_second) * gradient * gradient
    first_hat = first_new / (1.0 - beta_first**STEP)
    second_hat = second_new / (1.0 - beta_second**STEP)
    updated = master - step_rate * (
        first_hat / (jnp.sqrt(second_hat) + adam_eps) + weight_decay * master
    )
    return (updated, first_new, second_new, updated.astype(jnp.bfloat16))


class Links:
    def __init__(self, seqs, copies):
        self.seqs, self.copies, self.ring = seqs, copies, copies // 2
        self.s = lax.axis_index("seq")
        position = lax.axis_index("dp")
        self.z, self.c = position // 2, position % 2

    def swap(self, array, seq=0, ring=0, core=0):
        pairs = [
            (s * self.copies + d, (s ^ seq) * self.copies + (d ^ (2 * ring + core)))
            for s in range(self.seqs)
            for d in range(self.copies)
        ]
        return lax.ppermute(array, AXES, pairs)

    def by_core(self, first, second):
        return (
            jnp.where(self.c == 0, first, second),
            jnp.where(self.c == 0, second, first),
        )

    def aligned(self, rows):
        return (2 * rows) % 16 == 0

    def gather(self, first, second):
        rows, half = first.shape
        own, other = self.by_core(first, second)
        given = self.swap(other, core=1)
        unit = jnp.concatenate(self.by_core(own, given), axis=0)
        units = [unit] + [self.swap(unit, ring=m) for m in range(1, self.ring)]
        if self.aligned(rows):
            block = jnp.stack(units)
        else:
            block = jnp.zeros((self.ring, 2 * rows, half), unit.dtype)
            for m, piece in enumerate(units):
                block = lax.dynamic_update_slice(
                    block, piece[None], (self.z ^ m, jnp.int32(0), jnp.int32(0))
                )
            block = block.reshape(1, self.ring * 2 * rows, half)
        blocks = [block] + [self.swap(block, seq=k) for k in range(1, self.seqs)]
        return blocks + [self.swap(piece, core=1) for piece in blocks]

    def reduce(self, keep, send, rows):
        given = self.swap(send, core=1)
        half = keep.shape[-1]
        sums = [keep[k].astype(f32) + given[k].astype(f32) for k in range(self.seqs)]
        total = sums[0]
        for k in range(1, self.seqs):
            total = total + self.swap(sums[k].astype(bf16), seq=k).astype(f32)
        total = total.reshape(self.ring, 2 * rows, half)
        if self.aligned(rows):
            units = [total[m] for m in range(self.ring)]
        else:
            units = [
                lax.dynamic_index_in_dim(total, self.z ^ m, 0, keepdims=False)
                for m in range(self.ring)
            ]
        unit = units[0]
        for m in range(1, self.ring):
            unit = unit + self.swap(units[m].astype(bf16), ring=m).astype(f32)
        own, other = self.by_core(unit[:rows], unit[rows:])
        given = self.swap(other.astype(bf16), core=1).astype(f32)
        return jnp.concatenate(self.by_core(own, given), axis=1)


def shards(
    inputs,
    masked_positions,
    masked_grads,
    kernel_paths,
    attn_weight,
    out_weight,
    point_weight,
    depth_weight,
    gains,
    shifts,
    first_attn,
    first_out,
    first_point,
    first_depth,
    first_gains,
    first_shifts,
    second_attn,
    second_out,
    second_point,
    second_depth,
    second_gains,
    second_shifts,
):
    seq_count, part_tokens, width = inputs.shape
    seqs, copies = lax.axis_size("seq"), lax.axis_size("dp")
    devices = seqs * copies
    tokens = seqs * part_tokens
    blocks, rows, _ = attn_weight.shape
    taps = depth_weight.shape[1]
    scale = (width // HEADS) ** (-0.5)
    links = Links(seqs, copies)
    subs = links.ring if links.aligned(rows) else 1
    part_rows = width // (seqs * subs)
    half = 3 * width // 2
    place = links.s
    mine = jnp.minimum(place, seq_count - 1)
    live = (place < seq_count).astype(jnp.int32)
    own_paths = lax.dynamic_index_in_dim(kernel_paths, mine, 0, keepdims=False)
    meta = jnp.concatenate(
        [
            jnp.stack([place, links.z if subs > 1 else jnp.zeros_like(links.z), links.c]),
            own_paths,
            live[None],
        ]
    ).astype(jnp.int32)
    own_places = lax.dynamic_index_in_dim(masked_positions, mine, 0, keepdims=True)
    own_grads = lax.dynamic_index_in_dim(masked_grads, mine, 0, keepdims=False)

    small_local = jnp.concatenate([depth_weight, gains, shifts], axis=1).astype(bf16)
    small_all = lax.all_gather(small_local, AXES, axis=0, tiled=False)
    small_all = jnp.moveaxis(small_all, 0, 2).reshape(blocks, SMALL, width).astype(f32)
    small_all = jnp.pad(small_all, ((0, 0), (0, 2), (0, 0)))

    def sent_to(k):
        return lax.dynamic_index_in_dim(
            inputs, jnp.minimum(place ^ k, seq_count - 1), 0, keepdims=False
        )

    x_parts = [sent_to(0)] + [links.swap(sent_to(k), seq=k) for k in range(1, seqs)]

    attn_pieces, mix_pieces = [], []
    for b in range(blocks):
        low = attn_weight[b].astype(bf16)
        attn_pieces.append(links.gather(low[:, :half], low[:, half:]))
        low_out, low_point = out_weight[b].astype(bf16), point_weight[b].astype(bf16)
        cut = width // 2
        mix_pieces.append(
            links.gather(
                jnp.concatenate([low_out[:, :cut], low_point[:, :cut]], axis=1),
                jnp.concatenate([low_out[:, cut:], low_point[:, cut:]], axis=1),
            )
        )

    def shape(*dims, dtype=f32):
        return jax.ShapeDtypeStruct(dims, dtype)

    dma = pltpu.SemaphoreType.DMA
    square = (width, width)
    x_low, x_full = None, None
    saved = []
    for b in range(blocks):
        parts = x_parts if b == 0 else [x_low]
        x16, xt, qkv, o, ot, lse = call(
            partial(attend_kernel, len(parts), seqs, scale),
            (
                shape(tokens, width, dtype=bf16),
                shape(width, tokens, dtype=bf16),
                shape(tokens, 3 * width, dtype=bf16),
                shape(tokens, width, dtype=bf16),
                shape(width, tokens, dtype=bf16),
                shape(128, tokens),
            ),
            [smem_spec(), vmem_spec()]
            + [any_spec() if b == 0 else vmem_spec()] * len(parts)
            + [any_spec()] * (2 * seqs),
            [pltpu.VMEM((width, 3 * width), bf16), dma, dma],
            8 * 10**9,
            f"attend_{b}",
        )(meta, small_all[b], *parts, *attn_pieces[b])
        final = b == blocks - 1
        y, y_low, xh1, inv1, xh2, inv2, hct = call(
            partial(mix_kernel, b, seqs, taps, seqs if final else 0),
            (
                shape(8, 128) if final else shape(tokens, width),
                shape(seqs, part_tokens, width, dtype=bf16)
                if final
                else shape(tokens, width, dtype=bf16),
                shape(tokens, width),
                shape(tokens, 1),
                shape(tokens, width),
                shape(tokens, 1),
                shape(width, tokens, dtype=bf16),
            ),
            [smem_spec()] + [vmem_spec()] * 3 + [any_spec()] * (2 * seqs),
            [
                pltpu.VMEM(square, bf16),
                pltpu.VMEM(square, bf16),
                pltpu.VMEM((tokens, width), f32),
                pltpu.VMEM((tokens, width), f32),
                pltpu.VMEM((tokens + 2 * PAD, width), f32),
                pltpu.VMEM((tokens, width), bf16),
                dma,
            ],
            8 * 10**9,
            f"mix_{b}",
        )(meta, small_all[b], x16 if b == 0 else x_full, o, *mix_pieces[b])
        saved.append((xt, qkv, ot, lse, xh1, inv1, xh2, inv2, hct))
        x_low, x_full = y_low, y

    def sent_back(array):
        stacked = [array[0]] + [links.swap(array[k], seq=k) for k in range(1, seqs)]
        stacked = jnp.stack(stacked)
        return jnp.stack(
            [
                lax.dynamic_index_in_dim(stacked, place ^ i, 0, keepdims=False)
                for i in range(seq_count)
            ]
        )

    result = sent_back(x_low)
    dy = None
    big = [None] * blocks
    small_grads = [None] * blocks
    for b in reversed(range(blocks)):
        xt, qkv, ot, lse, xh1, inv1, xh2, inv2, hct = saved[b]
        last = b == blocks - 1
        upstream = (own_places, own_grads) if last else (dy,)
        dr1, do, keep, send, sums = call(
            partial(unmix_kernel, b, seqs, taps, last),
            (
                shape(tokens, width),
                shape(tokens, width, dtype=bf16),
                shape(seqs, subs, part_rows, width, dtype=bf16),
                shape(seqs, subs, part_rows, width, dtype=bf16),
                shape(16, width),
            ),
            [smem_spec()] + [vmem_spec()] * (len(upstream) + 7) + [any_spec()] * (2 * seqs),
            [
                pltpu.VMEM(square, bf16),
                pltpu.VMEM(square, bf16),
                pltpu.VMEM((tokens, width), f32),
                pltpu.VMEM((tokens, width), bf16),
                pltpu.VMEM((tokens + 2 * PAD, width), f32),
                pltpu.VMEM((tokens + 2 * PAD, width), f32),
                dma,
            ],
            12 * 10**9,
            f"unmix_{b}",
        )(meta, small_all[b], *upstream, xh2, inv2, xh1, inv1, hct, ot, *mix_pieces[b])
        grad_mix = links.reduce(keep, send, rows)
        dqkv, keep, send, bias = call(
            partial(unattend_kernel, scale),
            (
                shape(tokens, 3 * width, dtype=bf16),
                shape(seqs, subs, part_rows, half, dtype=bf16),
                shape(seqs, subs, part_rows, half, dtype=bf16),
                shape(1, width),
            ),
            [smem_spec()] + [vmem_spec()] * 4,
            [],
            16 * 10**9,
            f"unattend_{b}",
        )(meta, qkv, do, lse, xt)
        grad_attn = links.reduce(keep, send, rows)
        dy = call(
            partial(unproject_kernel, seqs, 0 if b else seqs),
            shape(tokens, width) if b else shape(seqs, part_tokens, width, dtype=bf16),
            [smem_spec()] + [vmem_spec()] * 2 + [any_spec()] * (2 * seqs),
            [pltpu.VMEM((width, 3 * width), bf16), dma],
            6 * 10**9,
            f"unproject_{b}",
        )(meta, dqkv, dr1, *attn_pieces[b])
        cut = width // 2
        big[b] = (
            grad_attn,
            jnp.concatenate([grad_mix[:, :cut], grad_mix[:, width : width + cut]], axis=1),
            jnp.concatenate([grad_mix[:, cut:width], grad_mix[:, width + cut :]], axis=1),
        )
        small_grads[b] = jnp.concatenate([sums[: SHIFT + 2], bias, sums[SHIFT + 3 : SMALL]])
    input_grad = sent_back(dy).astype(f32)

    small_sum = jnp.stack(small_grads).reshape(blocks * SMALL, devices, width // devices)
    small_sum = lax.psum_scatter(
        jnp.moveaxis(small_sum, 1, 0).reshape(devices, -1), AXES, scatter_dimension=0, tiled=True
    ).reshape(blocks, SMALL, width // devices)
    reduced = (
        jnp.stack([big[b][0] for b in range(blocks)]),
        jnp.stack([big[b][1] for b in range(blocks)]),
        jnp.stack([big[b][2] for b in range(blocks)]),
        small_sum[:, :taps],
        small_sum[:, GAIN:SHIFT],
        small_sum[:, SHIFT:SMALL],
    )
    masters = (attn_weight, out_weight, point_weight, depth_weight, gains, shifts)
    firsts = (first_attn, first_out, first_point, first_depth, first_gains, first_shifts)
    seconds = (second_attn, second_out, second_point, second_depth, second_gains, second_shifts)
    rates = (rate_attn, rate_out, rate_point, rate_depth, rate_gain, rate_vector)
    updates = [
        adam_update(
            masters[member], firsts[member], seconds[member], reduced[member], rates[member]
        )
        for member in range(6)
    ]
    return (
        (result, input_grad)
        + tuple((entry[0] for entry in updates))
        + tuple((entry[1] for entry in updates))
        + tuple((entry[2] for entry in updates))
        + tuple((entry[3] for entry in updates))
    )


def solution(mesh):
    sequence = P("dp", "seq", None)
    matrix = P(None, AXES, None)
    vector = P(None, None, AXES)
    weights = (matrix,) * 3 + (vector,) * 3
    return jax.shard_map(
        shards,
        mesh=mesh,
        in_specs=(sequence, P("dp", None), P("dp", None, None), P("dp", None)) + weights * 3,
        out_specs=(sequence, sequence) + weights * 4,
        check_vma=False,
    )
```

time: 1100 us -> 539 us (0.49)
  waiting for transfers between devices: 609 us -> 232 us
  Pallas kernels: 0 us -> 129 us
  local copies, waits for them, and re-layouts: 138 us -> 22.1 us
  blocking collectives: 148 us -> 41.1 us
  matrix products: 106 us -> 0 us
  starting transfers between devices: 21.3 us -> 78.8 us
  other arithmetic: 45.6 us -> 12.5 us
    unnamed x27 -> x2, waiting for transfers between devices: 309 us -> 108 us
    all_gather x7 -> x0, waiting for transfers between devices: 145 us -> none  [the longest x1 78.1 us: shards(): lax.all_gather(attn_weight.astype(jnp.bfloat16), ('seq', 'dp'), axis=1, t...]
    reduce_scatter x6 -> x0, waiting for transfers between devices: 143 us -> none  [the longest x2 75.3 us: shards(): lax.psum_scatter(grad_key_part.reshape(seq_count, -1, model_width).astype...]
    pallas_call x0 -> x10, Pallas kernels: none -> 129 us  [the longest x2 32.2 us: shards(): call(partial(unattend_kernel, scale), (shape(tokens, 3 * width, dtype=bf1...]
    ppermute x8 -> x85, waiting for transfers between devices: 12.2 us -> 124 us  [swap(): return lax.ppermute(array, AXES, pairs)]
    dot_general x31 -> x0, matrix products: 106 us -> none  [the longest x2 14.4 us: attend_backward(): jnp.einsum('phtl,pthe->plhe', attn_probs.astype(jnp.bfloat16), grad_heads...]
    all_gather x3 -> x1, blocking collectives: 120 us -> 41.1 us  [shards(): small_all = lax.all_gather(small_local, AXES, axis=0, tiled=False)]
    ppermute x8 -> x85, starting transfers between devices: 19.8 us -> 78.8 us  [swap(): return lax.ppermute(array, AXES, pairs)]
  transfers between devices with their start and end apart: 28 -> 86, of which waited for: 21 -> 30; matrix products, arithmetic and copies ran while one was open for 18% -> 5% of each run, Pallas kernels for 0% -> 22%
where the time goes in v1:
time: 539 us; the launch traced here: 531 us
  waiting for transfers between devices  232 us (43%)
  Pallas kernels  129 us (24%)
  starting transfers between devices  78.8 us (15%)
  blocking collectives  41.1 us (8%)
  local copies, waits for them, and re-layouts  22.1 us (4%)
  between operations  15.6 us (3%)
  other arithmetic  12.5 us (2%)
    ppermute x85, waiting for transfers between devices, swap(): return lax.ppermute(array, AXES, pairs)  124 us
    unnamed x2, waiting for transfers between devices  108 us
    ppermute x85, starting transfers between devices, swap(): return lax.ppermute(array, AXES, pairs)  78.8 us
    all_gather x1, blocking collectives, shards(): small_all = lax.all_gather(small_local, AXES, axis=0, tiled=False)  41.1 us
    pallas_call x2, Pallas kernels, shards(): call(partial(unattend_kernel, scale), (shape(tokens, 3 * width, dtype=bf1...  32.2 us
    pallas_call x2, Pallas kernels, shards(): call(partial(unmix_kernel, b, seqs, taps, last), (shape(tokens, width), s...  31.7 us
    pallas_call x2, Pallas kernels, shards(): call(partial(mix_kernel, b, seqs, taps, seqs if final else 0), (shape(8,...  26.8 us
    pallas_call x2, Pallas kernels, shards(): call(partial(attend_kernel, len(parts), seqs, scale), (shape(tokens, widt...  23.4 us
  transfers between devices with their start and end apart: 86, of which 30 were waited for; matrix products, arithmetic and copies ran while one was open for 5% of the time, Pallas kernels for 22%

profile of v1, /device:TPU:0, one launch (start us, length us, event | category | flops | bytes accessed | tf_op | source)
XLA Modules:
  0.0 530.7 jit_solution(5143679030287463216)
XLA Ops:
  11.8 5.1 collective-permute-start.17
  17.6 3.8 collective-permute-start.39
  24.0 3.1 collective-permute-done.16
  30.7 4.4 collective-permute-done.38
  45.6 3.5 collective-permute-done.27
  50.3 41.1 %all_gather.4 = bf16[32,2,14,24]{3,1,2,0:T(2,128)(2,1)S(1)} all-gather(bf16[1,2,14,24]{3,1,2,0:T(2,128)(2,1)S(1)} %pad_maximum_fusion.19), channel_id=1, replica_groups=mesh['seq'=4,'dp'=8] {'seq','dp'}, dimensions={0}, use_global_device_ids=true | all-gather | bytes 44352 | tf_op jit(solution)/shard_map/all_gather | solution.py:534
  94.8 5.6 %collective-permute-done.2.refs_3_ = bf16[128,768]{1,0:T(8,128)(2,1)S(1)} collective-permute-done((bf16[128,768]{1,0:T(8,128)(2,1)S(1)}, bf16[128,768]{1,0:T(8,128)(2,1)S(1)}, u32[]{:S(2)}, u32[]{:S(2)}) %collective-permute-start.2) | collective-permute-done | bytes 196640 | tf_op jit(solution)/shard_map/ppermute | solution.py:432
  109.7 21.6 %collective-permute-done.40.refs_1_.refs_9_ = bf16[4,48,768]{2,1,0:T(8,128)(2,1)S(1)} collective-permute-done((bf16[4,48,768]{2,1,0:T(8,128)(2,1)S(1)}, bf16[4,48,768]{2,1,0:T(8,128)(2,1)S(1)}, u32[]{:S(2)}, u32[]{:S(2)}) %collective-permute-start.40) | collective-permute-done | bytes 294944 | tf_op jit(solution)/shard_map/ppermute | solution.py:432
  135.9 7.9 %collective-permute-done.29.refs_2_.refs_1_ = bf16[4,48,1152]{2,1,0:T(8,128)(2,1)S(1)} collective-permute-done((bf16[4,48,1152]{2,1,0:T(8,128)(2,1)S(1)}, bf16[4,48,1152]{2,1,0:T(8,128)(2,1)S(1)}, u32[]{:S(2)}, u32[]{:S(2)}) %collective-permute-start.29) | collective-permute-done | bytes 442400 | tf_op jit(solution)/shard_map/ppermute | solution.py:432
  145.9 11.7 %attend_0.1 = (bf16[512,768]{1,0:T(8,128)(2,1)}, bf16[768,512]{1,0:T(8,128)(2,1)}, bf16[512,2304]{1,0:T(8,128)(2,1)}, bf16[512,768]{1,0:T(8,128)(2,1)}, bf16[768,512]{1,0:T(8,128)(2,1)}, /*index=5*/f32[128,512]{1,0:T(8,128)}) custom-call(s32[6]{0:T(128)} %concatenate.68.meta, f32[16,768]{1,0:T(8,128)} %get-tuple-element.284.small, ...), custom_call_target="tpu_custom_call" | custom-call | flops 8000000000 | bytes 4194304 | tf_op jit(solution)/shard_map/attend_0/pallas_call | solution.py:567
  161.4 13.8 %mix_0.1 = (f32[512,768]{1,0:T(8,128)}, bf16[512,768]{1,0:T(8,128)(2,1)}, f32[512,768]{1,0:T(8,128)}, f32[512,1]{1,0:T(8,128)}, f32[512,768]{1,0:T(8,128)}, /*index=5*/f32[512,1]{1,0:T(8,128)}, bf16[768,512]{1,0:T(8,128)(2,1)}) custom-call(s32[6]{0:T(128)} %concatenate.68.meta, f32[16,768]{1,0:T(8,128)} %get-tuple-element.284.small, ...), custom_call_target="tpu_custom_call" | custom-call | flops 8000000000 | bytes 4194304 | tf_op jit(solution)/shard_map/mix_0/pallas_call | solution.py:585
  177.2 11.6 %attend_1.1 = (bf16[512,768]{1,0:T(8,128)(2,1)}, bf16[768,512]{1,0:T(8,128)(2,1)}, bf16[512,2304]{1,0:T(8,128)(2,1)}, bf16[512,768]{1,0:T(8,128)(2,1)}, bf16[768,512]{1,0:T(8,128)(2,1)}, /*index=5*/f32[128,512]{1,0:T(8,128)}) custom-call(s32[6]{0:T(128)} %concatenate.68.meta, f32[16,768]{1,0:T(8,128)} %get-tuple-element.285.small, ...), custom_call_target="tpu_custom_call" | custom-call | flops 8000000000 | bytes 4194304 | tf_op jit(solution)/shard_map/attend_1/pallas_call | solution.py:567
  189.9 13.1 %mix_1.1 = (f32[8,128]{1,0:T(8,128)}, bf16[4,128,768]{2,1,0:T(8,128)(2,1)}, f32[512,768]{1,0:T(8,128)}, f32[512,1]{1,0:T(8,128)}, f32[512,768]{1,0:T(8,128)}, /*...) custom-call(s32[6]{0:T(128)} %concatenate.68.meta, f32[16,768]{1,0:T(8,128)} %get-tuple-element.285.small, ...), custom_call_target="tpu_custom_call" | custom-call | flops 8000000000 | bytes 4194304 | tf_op jit(solution)/shard_map/mix_1/pallas_call | solution.py:585
  208.5 15.8 %unmix_1.1 = (f32[512,768]{1,0:T(8,128)}, bf16[512,768]{1,0:T(8,128)(2,1)}, bf16[4,4,48,768]{3,2,1,0:T(8,128)(2,1)}, bf16[4,4,48,768]{3,2,1,0:T(8,128)(2,1)}, f32[16,768]{1,0:T(8,128)}) custom-call(s32[6]{0:T(128)} %concatenate.68.meta, f32[16,768]{1,0:T(8,128)} %get-tuple-element.285.small, s32[1,76]{1,0:T(1,128)} %constant_dynamic-slice_fusion.3.refs_0_, ...), custom_call_target="tpu_custom_call" | custom-call | flops 12000000000 | bytes 4194304 | tf_op jit(solution)/shard_map/unmix_1/pallas_call | solution.py:632
  225.1 16.1 %unattend_1.1 = (bf16[512,2304]{1,0:T(8,128)(2,1)}, bf16[4,4,48,1152]{3,2,1,0:T(8,128)(2,1)}, bf16[4,4,48,1152]{3,2,1,0:T(8,128)(2,1)}, f32[1,768]{1,0:T(1,128)}) custom-call(s32[6]{0:T(128)} %concatenate.68.meta, bf16[512,2304]{1,0:T(8,128)(2,1)} %get-tuple-element.75.qkv, bf16[512,768]{1,0:T(8,128)(2,1)} %get-tuple-element.82.do_ref, ...), custom_call_target="tpu_custom_call" | custom-call | flops 16000000000 | bytes 4194304 | tf_op jit(solution)/shard_map/unattend_1/pallas_call | solution.py:655
  241.2 7.8 %unproject_1.1.refs_0_ = f32[512,768]{1,0:T(8,128)} custom-call(s32[6]{0:T(128)} %concatenate.68.meta, bf16[512,2304]{1,0:T(8,128)(2,1)} %get-tuple-element.85.dqkv, f32[512,768]{1,0:T(8,128)} %get-tuple-element.86.dr1, bf16[4,48,1152]{2,1,0:T(8,128)(2,1)} %copy-done.13, bf16[4,48,1152]{2,1,0:T(8,128)(2,1)} %copy-done.39, bf16[4,48,1152]{2,1,0:T(8,128)(2,1)} %copy-done.40, ...), custom_call_target="tpu_custom_call" | custom-call | flops 6000000000 | bytes 4194304 | tf_op jit(solution)/shard_map/unproject_1/pallas_call | solution.py:669
  249.0 15.8 %unmix_0.1 = (f32[512,768]{1,0:T(8,128)}, bf16[512,768]{1,0:T(8,128)(2,1)}, bf16[4,4,48,768]{3,2,1,0:T(8,128)(2,1)}, bf16[4,4,48,768]{3,2,1,0:T(8,128)(2,1)}, f32[16,768]{1,0:T(8,128)}) custom-call(s32[6]{0:T(128)} %concatenate.68.meta, f32[16,768]{1,0:T(8,128)} %get-tuple-element.284.small, f32[512,768]{1,0:T(8,128)} %unproject_1.1.refs_0_, ...), custom_call_target="tpu_custom_call" | custom-call | flops 12000000000 | bytes 4194304 | tf_op jit(solution)/shard_map/unmix_0/pallas_call | solution.py:632
  265.6 16.1 %unattend_0.1 = (bf16[512,2304]{1,0:T(8,128)(2,1)}, bf16[4,4,48,1152]{3,2,1,0:T(8,128)(2,1)}, bf16[4,4,48,1152]{3,2,1,0:T(8,128)(2,1)}, f32[1,768]{1,0:T(1,128)}) custom-call(s32[6]{0:T(128)} %concatenate.68.meta, bf16[512,2304]{1,0:T(8,128)(2,1)} %get-tuple-element.74.qkv, bf16[512,768]{1,0:T(8,128)(2,1)} %get-tuple-element.93.do_ref, ...), custom_call_target="tpu_custom_call" | custom-call | flops 16000000000 | bytes 4194304 | tf_op jit(solution)/shard_map/unattend_0/pallas_call | solution.py:655
  284.1 7.1 %unproject_0.1 = bf16[4,128,768]{2,1,0:T(8,128)(2,1)} custom-call(s32[6]{0:T(128)} %concatenate.68.meta, bf16[512,2304]{1,0:T(8,128)(2,1)} %get-tuple-element.96.dqkv, f32[512,768]{1,0:T(8,128)} %get-tuple-element.97.dr1, bf16[4,48,1152]{2,1,0:T(8,128)(2,1)} %copy-done.12, bf16[4,48,1152]{2,1,0:T(8,128)(2,1)} %collective-permute-done.7.refs_5_.refs_1_, ...), custom_call_target="tpu_custom_call" | custom-call | flops 6000000000 | bytes 4194304 | tf_op jit(solution)/shard_map/unproject_0/pallas_call | solution.py:669
  293.9 107.7 %all-reduce.4.cloned.1.call-done = f32[32,672]{1,0:T(8,128)} async-done(((f32[32,672]{1,0:T(8,128)}), f32[32,672]{1,0:T(8,128)}) %all-reduce.4.cloned.1.call-update) | async-done | bytes 86032
  412.4 4.4 collective-permute-done.52
  426.3 6.2 %collective-permute-done.80 = bf16[4,48,768]{2,1,0:T(8,128)(2,1)S(1)} collective-permute-done((bf16[4,48,768]{2,1,0:T(8,128)(2,1)S(1)}, bf16[4,48,768]{2,1,0:T(8,128)(2,1)S(1)}, u32[]{:S(2)}, u32[]{:S(2)}) %collective-permute-start.80) | collective-permute-done | bytes 294944 | tf_op jit(solution)/shard_map/ppermute | solution.py:432
  434.0 4.8 collective-permute-done.79
  441.0 4.2 collective-permute-done.72
  447.0 3.4 collective-permute-done.71
  460.1 3.4 collective-permute-done.74
  473.9 7.2 %collective-permute-done.64 = bf16[4,48,1152]{2,1,0:T(8,128)(2,1)S(1)} collective-permute-done((bf16[4,48,1152]{2,1,0:T(8,128)(2,1)S(1)}, bf16[4,48,1152]{2,1,0:T(8,128)(2,1)S(1)}, u32[]{:S(2)}, u32[]{:S(2)}) %collective-permute-start.64) | collective-permute-done | bytes 442400 | tf_op jit(solution)/shard_map/ppermute | solution.py:432
  482.5 8.1 %collective-permute-done.63 = bf16[4,48,1152]{2,1,0:T(8,128)(2,1)S(1)} collective-permute-done((bf16[4,48,1152]{2,1,0:T(8,128)(2,1)S(1)}, bf16[4,48,1152]{2,1,0:T(8,128)(2,1)S(1)}, u32[]{:S(2)}, u32[]{:S(2)}) %collective-permute-start.63) | collective-permute-done | bytes 442400 | tf_op jit(solution)/shard_map/ppermute | solution.py:432
  493.2 6.8 %collective-permute-done.56 = bf16[4,48,1152]{2,1,0:T(8,128)(2,1)S(1)} collective-permute-done((bf16[4,48,1152]{2,1,0:T(8,128)(2,1)S(1)}, bf16[4,48,1152]{2,1,0:T(8,128)(2,1)S(1)}, u32[]{:S(2)}, u32[]{:S(2)}) %collective-permute-start.56) | collective-permute-done | bytes 442400 | tf_op jit(solution)/shard_map/ppermute | solution.py:432
  500.1 8.5 %collective-permute-done.55 = bf16[4,48,1152]{2,1,0:T(8,128)(2,1)S(1)} collective-permute-done((bf16[4,48,1152]{2,1,0:T(8,128)(2,1)S(1)}, bf16[4,48,1152]{2,1,0:T(8,128)(2,1)S(1)}, u32[]{:S(2)}, u32[]{:S(2)}) %collective-permute-start.55) | collective-permute-done | bytes 442400 | tf_op jit(solution)/shard_map/ppermute | solution.py:432
  513.7 3.2 collective-permute-done.59
  516.9 3.8 collective-permute-done.58
  (376 shorter events, 118.3 us)
Async XLA Ops:
  7.3 394.3 %all-reduce.4.cloned.1.call-start = ((), (), s32[]{:S(2)}) async-start(), calls=%async_computation | async-start | bytes 196608
  29.1 62.6 %collective-permute-start = (bf16[128,768]{1,0:T(8,128)(2,1)S(1)}, bf16[128,768]{1,0:T(8,128)(2,1)S(1)}, u32[]{:S(2)}, u32[]{:S(2)}) collective-permute-start(bf16[128,768]{1,0:T(8,128)(2,1)S(1)} %get-tuple-element.247), channel_id=1, source_target_pairs={{0,8},{1,9},{2,10},{3,11},{4,12},{5,13},{6,14},{7,15},{8,0},{9,1},... | collective-permute-start | bytes 589832 | tf_op jit(solution)/shard_map/ppermute | solution.py:432
  35.1 59.6 %collective-permute-start.1 = (bf16[128,768]{1,0:T(8,128)(2,1)S(1)}, bf16[128,768]{1,0:T(8,128)(2,1)}, u32[]{:S(2)}, u32[]{:S(2)}) collective-permute-start(bf16[128,768]{1,0:T(8,128)(2,1)S(1)} %get-tuple-element.249), channel_id=1, source_target_pairs={{0,16},{1,17},{2,18},{3,19},{4,20},{5,21},{6,22},{7,23},{8,24},{9,... | collective-permute-start | bytes 589832 | tf_op jit(solution)/shard_map/ppermute | solution.py:432
  41.8 49.9 %collective-permute-start.26 = (bf16[48,1152]{1,0:T(8,128)(2,1)S(1)}, bf16[48,1152]{1,0:T(8,128)(2,1)S(1)}, u32[]{:S(2)}, u32[]{:S(2)}) collective-permute-start(bf16[48,1152]{1,0:T(8,128)(2,1)S(1)} %get-tuple-element.279), channel_id=1, source_target_pairs={{0,2},{1,3},{2,0},{3,1},{4,6},{5,7},{6,4},{7,5},{8,10},{9,11},{10,... | collective-permute-start | bytes 331784 | tf_op jit(solution)/shard_map/ppermute | solution.py:432
  44.2 56.2 %collective-permute-start.18 = (bf16[4,48,768]{2,1,0:T(8,128)(2,1)S(1)}, bf16[4,48,768]{2,1,0:T(8,128)(2,1)}, u32[]{:S(2)}, u32[]{:S(2)}) collective-permute-start(bf16[4,48,768]{2,1,0:T(8,128)(2,1)S(1)} %pad_maximum_fusion.6.refs_0_.refs_7_), channel_id=1, source_target_pairs={{0,8},{1,9},{2,10},{3,11},{4,12},{5,13},{6,14},{7,15},{8,0},{9,1},... | collective-permute-start | bytes 884744 | tf_op jit(solution)/shard_map/ppermute | solution.py:432
  49.1 52.6 %collective-permute-start.19 = (bf16[4,48,768]{2,1,0:T(8,128)(2,1)S(1)}, bf16[4,48,768]{2,1,0:T(8,128)(2,1)}, u32[]{:S(2)}, u32[]{:S(2)}) collective-permute-start(bf16[4,48,768]{2,1,0:T(8,128)(2,1)S(1)} %pad_maximum_fusion.6.refs_0_.refs_7_), channel_id=1, source_target_pairs={{0,16},{1,17},{2,18},{3,19},{4,20},{5,21},{6,22},{7,23},{8,24},{9,... | collective-permute-start | bytes 884744 | tf_op jit(solution)/shard_map/ppermute | solution.py:432
  100.4 31.6 %collective-permute-start.7 = (bf16[4,48,1152]{2,1,0:T(8,128)(2,1)S(1)}, bf16[4,48,1152]{2,1,0:T(8,128)(2,1)}, u32[]{:S(2)}, u32[]{:S(2)}) collective-permute-start(bf16[4,48,1152]{2,1,0:T(8,128)(2,1)S(1)} %pad_maximum_fusion.3.refs_4_.refs_0_), channel_id=1, source_target_pairs={{0,8},{1,9},{2,10},{3,11},{4,12},{5,13},{6,14},{7,15},{8,0},{9,1},... | collective-permute-start | bytes 1327112 | tf_op jit(solution)/shard_map/ppermute | solution.py:432
  100.4 31.6 %collective-permute-start.8 = (bf16[4,48,1152]{2,1,0:T(8,128)(2,1)S(1)}, bf16[4,48,1152]{2,1,0:T(8,128)(2,1)}, u32[]{:S(2)}, u32[]{:S(2)}) collective-permute-start(bf16[4,48,1152]{2,1,0:T(8,128)(2,1)S(1)} %pad_maximum_fusion.3.refs_4_.refs_0_), channel_id=1, source_target_pairs={{0,16},{1,17},{2,18},{3,19},{4,20},{5,21},{6,22},{7,23},{8,24},{9,... | collective-permute-start | bytes 1327112 | tf_op jit(solution)/shard_map/ppermute | solution.py:432
  101.7 30.8 %collective-permute-start.9 = (bf16[4,48,1152]{2,1,0:T(8,128)(2,1)S(1)}, bf16[4,48,1152]{2,1,0:T(8,128)(2,1)}, u32[]{:S(2)}, u32[]{:S(2)}) collective-permute-start(bf16[4,48,1152]{2,1,0:T(8,128)(2,1)S(1)} %pad_maximum_fusion.3.refs_4_.refs_0_), channel_id=1, source_target_pairs={{0,24},{1,25},{2,26},{3,27},{4,28},{5,29},{6,30},{7,31},{8,16},{9,... | collective-permute-start | bytes 1327112 | tf_op jit(solution)/shard_map/ppermute | solution.py:432
  106.7 24.5 %collective-permute-start.40 = (bf16[4,48,768]{2,1,0:T(8,128)(2,1)S(1)}, bf16[4,48,768]{2,1,0:T(8,128)(2,1)S(1)}, u32[]{:S(2)}, u32[]{:S(2)}) collective-permute-start(bf16[4,48,768]{2,1,0:T(8,128)(2,1)S(1)} %pad_maximum_fusion.7.refs_0_.refs_8_), channel_id=1, source_target_pairs={{0,8},{1,9},{2,10},{3,11},{4,12},{5,13},{6,14},{7,15},{8,0},{9,1},... | collective-permute-start | bytes 884744 | tf_op jit(solution)/shard_map/ppermute | solution.py:432
  107.5 24.0 %collective-permute-start.41 = (bf16[4,48,768]{2,1,0:T(8,128)(2,1)S(1)}, bf16[4,48,768]{2,1,0:T(8,128)(2,1)}, u32[]{:S(2)}, u32[]{:S(2)}) collective-permute-start(bf16[4,48,768]{2,1,0:T(8,128)(2,1)S(1)} %pad_maximum_fusion.7.refs_0_.refs_8_), channel_id=1, source_target_pairs={{0,16},{1,17},{2,18},{3,19},{4,20},{5,21},{6,22},{7,23},{8,24},{9,... | collective-permute-start | bytes 884744 | tf_op jit(solution)/shard_map/ppermute | solution.py:432
  135.1 22.5 %collective-permute-start.30 = (bf16[4,48,1152]{2,1,0:T(8,128)(2,1)S(1)}, bf16[4,48,1152]{2,1,0:T(8,128)(2,1)S(1)}, u32[]{:S(2)}, u32[]{:S(2)}) collective-permute-start(bf16[4,48,1152]{2,1,0:T(8,128)(2,1)S(1)} %pad_maximum_fusion.4.refs_1_.refs_0_), channel_id=1, source_target_pairs={{0,16},{1,17},{2,18},{3,19},{4,20},{5,21},{6,22},{7,23},{8,24},{9,... | collective-permute-start | bytes 1327112 | tf_op jit(solution)/shard_map/ppermute | solution.py:432
  143.9 16.1 %collective-permute-start.31 = (bf16[4,48,1152]{2,1,0:T(8,128)(2,1)S(1)}, bf16[4,48,1152]{2,1,0:T(8,128)(2,1)S(1)}, u32[]{:S(2)}, u32[]{:S(2)}) collective-permute-start(bf16[4,48,1152]{2,1,0:T(8,128)(2,1)S(1)} %pad_maximum_fusion.4.refs_1_.refs_0_), channel_id=1, source_target_pairs={{0,24},{1,25},{2,26},{3,27},{4,28},{5,29},{6,30},{7,31},{8,16},{9,... | collective-permute-start | bytes 1327112 | tf_op jit(solution)/shard_map/ppermute | solution.py:432
  144.6 16.0 %collective-permute-start.23 = (bf16[4,48,768]{2,1,0:T(8,128)(2,1)}, bf16[4,48,768]{2,1,0:T(8,128)(2,1)S(1)}, u32[]{:S(2)}, u32[]{:S(2)}) collective-permute-start(bf16[4,48,768]{2,1,0:T(8,128)(2,1)} %collective-permute-done.19.refs_2_.refs_9_), channel_id=1, source_target_pairs={{0,1},{1,0},{2,3},{3,2},{4,5},{5,4},{6,7},{7,6},{8,9},{9,8},{10,11... | collective-permute-start | bytes 884744 | tf_op jit(solution)/shard_map/ppermute | solution.py:432
  157.6 17.6 %collective-permute-start.42 = (bf16[4,48,768]{2,1,0:T(8,128)(2,1)S(1)}, bf16[4,48,768]{2,1,0:T(8,128)(2,1)S(1)}, u32[]{:S(2)}, u32[]{:S(2)}) collective-permute-start(bf16[4,48,768]{2,1,0:T(8,128)(2,1)S(1)} %pad_maximum_fusion.7.refs_0_.refs_8_), channel_id=1, source_target_pairs={{0,24},{1,25},{2,26},{3,27},{4,28},{5,29},{6,30},{7,31},{8,16},{9,... | collective-permute-start | bytes 884744 | tf_op jit(solution)/shard_map/ppermute | solution.py:432
  159.9 15.8 %collective-permute-start.32 = (bf16[4,48,1152]{2,1,0:T(8,128)(2,1)S(1)}, bf16[4,48,1152]{2,1,0:T(8,128)(2,1)S(1)}, u32[]{:S(2)}, u32[]{:S(2)}) collective-permute-start(bf16[4,48,1152]{2,1,0:T(8,128)(2,1)S(1)} %pad_maximum_fusion.4.refs_1_.refs_0_), channel_id=1, source_target_pairs={{0,1},{1,0},{2,3},{3,2},{4,5},{5,4},{6,7},{7,6},{8,9},{9,8},{10,11... | collective-permute-start | bytes 1327112 | tf_op jit(solution)/shard_map/ppermute | solution.py:432
  160.0 15.8 %collective-permute-start.33 = (bf16[4,48,1152]{2,1,0:T(8,128)(2,1)S(1)}, bf16[4,48,1152]{2,1,0:T(8,128)(2,1)S(1)}, u32[]{:S(2)}, u32[]{:S(2)}) collective-permute-start(bf16[4,48,1152]{2,1,0:T(8,128)(2,1)S(1)} %collective-permute-done.29.refs_2_.refs_1_), channel_id=1, source_target_pairs={{0,1},{1,0},{2,3},{3,2},{4,5},{5,4},{6,7},{7,6},{8,9},{9,8},{10,11... | collective-permute-start | bytes 1327112 | tf_op jit(solution)/shard_map/ppermute | solution.py:432
  160.7 15.7 %collective-permute-start.35 = (bf16[4,48,1152]{2,1,0:T(8,128)(2,1)S(1)}, bf16[4,48,1152]{2,1,0:T(8,128)(2,1)S(1)}, u32[]{:S(2)}, u32[]{:S(2)}) collective-permute-start(bf16[4,48,1152]{2,1,0:T(8,128)(2,1)S(1)} %collective-permute-done.31.refs_4_.refs_3_), channel_id=1, source_target_pairs={{0,1},{1,0},{2,3},{3,2},{4,5},{5,4},{6,7},{7,6},{8,9},{9,8},{10,11... | collective-permute-start | bytes 1327112 | tf_op jit(solution)/shard_map/ppermute | solution.py:432
  205.0 202.8 %collective-permute-start.49 = (bf16[128,768]{1,0:T(8,128)(2,1)}, bf16[128,768]{1,0:T(8,128)(2,1)S(1)}, u32[]{:S(2)}, u32[]{:S(2)}) collective-permute-start(bf16[128,768]{1,0:T(8,128)(2,1)} %get-tuple-element.243), channel_id=1, source_target_pairs={{0,24},{1,25},{2,26},{3,27},{4,28},{5,29},{6,30},{7,31},{8,16},{9,... | collective-permute-start | bytes 589832 | tf_op jit(solution)/shard_map/ppermute | solution.py:432
  205.7 204.0 %collective-permute-start.48 = (bf16[128,768]{1,0:T(8,128)(2,1)}, bf16[128,768]{1,0:T(8,128)(2,1)S(1)}, u32[]{:S(2)}, u32[]{:S(2)}) collective-permute-start(bf16[128,768]{1,0:T(8,128)(2,1)} %get-tuple-element.244), channel_id=1, source_target_pairs={{0,16},{1,17},{2,18},{3,19},{4,20},{5,21},{6,22},{7,23},{8,24},{9,... | collective-permute-start | bytes 589832 | tf_op jit(solution)/shard_map/ppermute | solution.py:432
  206.8 204.0 %collective-permute-start.47 = (bf16[128,768]{1,0:T(8,128)(2,1)}, bf16[128,768]{1,0:T(8,128)(2,1)}, u32[]{:S(2)}, u32[]{:S(2)}) collective-permute-start(bf16[128,768]{1,0:T(8,128)(2,1)} %get-tuple-element.245), channel_id=1, source_target_pairs={{0,8},{1,9},{2,10},{3,11},{4,12},{5,13},{6,14},{7,15},{8,0},{9,1},... | collective-permute-start | bytes 589832 | tf_op jit(solution)/shard_map/ppermute | solution.py:432
  293.4 127.5 %collective-permute-start.77 = (bf16[4,4,48,768]{3,2,1,0:T(8,128)(2,1)}, bf16[4,4,48,768]{3,2,1,0:T(8,128)(2,1)S(1)}, u32[]{:S(2)}, u32[]{:S(2)}) collective-permute-start(bf16[4,4,48,768]{3,2,1,0:T(8,128)(2,1)} %get-tuple-element.105), channel_id=1, source_target_pairs={{0,1},{1,0},{2,3},{3,2},{4,5},{5,4},{6,7},{7,6},{8,9},{9,8},{10,11... | collective-permute-start | bytes 3538952 | tf_op jit(solution)/shard_map/ppermute | solution.py:432
  293.4 132.7 %collective-permute-start.69 = (bf16[4,4,48,768]{3,2,1,0:T(8,128)(2,1)}, bf16[4,4,48,768]{3,2,1,0:T(8,128)(2,1)S(1)}, u32[]{:S(2)}, u32[]{:S(2)}) collective-permute-start(bf16[4,4,48,768]{3,2,1,0:T(8,128)(2,1)} %get-tuple-element.103), channel_id=1, source_target_pairs={{0,1},{1,0},{2,3},{3,2},{4,5},{5,4},{6,7},{7,6},{8,9},{9,8},{10,11... | collective-permute-start | bytes 3538952 | tf_op jit(solution)/shard_map/ppermute | solution.py:432
  416.9 49.8 %collective-permute-start.61 = (bf16[4,4,48,1152]{3,2,1,0:T(8,128)(2,1)S(1)}, bf16[4,4,48,1152]{3,2,1,0:T(8,128)(2,1)S(1)}, u32[]{:S(2)}, u32[]{:S(2)}) collective-permute-start(bf16[4,4,48,1152]{3,2,1,0:T(8,128)(2,1)S(1)} %copy-done.33), channel_id=1, source_target_pairs={{0,1},{1,0},{2,3},{3,2},{4,5},{5,4},{6,7},{7,6},{8,9},{9,8},{10,11... | collective-permute-start | bytes 5308424 | tf_op jit(solution)/shard_map/ppermute | solution.py:432
  426.1 44.5 %collective-permute-start.53 = (bf16[4,4,48,1152]{3,2,1,0:T(8,128)(2,1)S(1)}, bf16[4,4,48,1152]{3,2,1,0:T(8,128)(2,1)S(1)}, u32[]{:S(2)}, u32[]{:S(2)}) collective-permute-start(bf16[4,4,48,1152]{3,2,1,0:T(8,128)(2,1)S(1)} %copy-done.34), channel_id=1, source_target_pairs={{0,1},{1,0},{2,3},{3,2},{4,5},{5,4},{6,7},{7,6},{8,9},{9,8},{10,11... | collective-permute-start | bytes 5308424 | tf_op jit(solution)/shard_map/ppermute | solution.py:432
  468.5 22.0 %collective-permute-start.63 = (bf16[4,48,1152]{2,1,0:T(8,128)(2,1)S(1)}, bf16[4,48,1152]{2,1,0:T(8,128)(2,1)S(1)}, u32[]{:S(2)}, u32[]{:S(2)}) collective-permute-start(bf16[4,48,1152]{2,1,0:T(8,128)(2,1)S(1)} %get-tuple-element.225), channel_id=1, source_target_pairs={{0,16},{1,17},{2,18},{3,19},{4,20},{5,21},{6,22},{7,23},{8,24},{9,... | collective-permute-start | bytes 1327112 | tf_op jit(solution)/shard_map/ppermute | solution.py:432
  470.0 20.6 %collective-permute-start.62 = (bf16[4,48,1152]{2,1,0:T(8,128)(2,1)S(1)}, bf16[4,48,1152]{2,1,0:T(8,128)(2,1)S(1)}, u32[]{:S(2)}, u32[]{:S(2)}) collective-permute-start(bf16[4,48,1152]{2,1,0:T(8,128)(2,1)S(1)} %get-tuple-element.223), channel_id=1, source_target_pairs={{0,8},{1,9},{2,10},{3,11},{4,12},{5,13},{6,14},{7,15},{8,0},{9,1},... | collective-permute-start | bytes 1327112 | tf_op jit(solution)/shard_map/ppermute | solution.py:432
  470.9 29.1 %collective-permute-start.56 = (bf16[4,48,1152]{2,1,0:T(8,128)(2,1)S(1)}, bf16[4,48,1152]{2,1,0:T(8,128)(2,1)S(1)}, u32[]{:S(2)}, u32[]{:S(2)}) collective-permute-start(bf16[4,48,1152]{2,1,0:T(8,128)(2,1)S(1)} %get-tuple-element.221), channel_id=1, source_target_pairs={{0,24},{1,25},{2,26},{3,27},{4,28},{5,29},{6,30},{7,31},{8,16},{9,... | collective-permute-start | bytes 1327112 | tf_op jit(solution)/shard_map/ppermute | solution.py:432
  472.4 36.2 %collective-permute-start.55 = (bf16[4,48,1152]{2,1,0:T(8,128)(2,1)S(1)}, bf16[4,48,1152]{2,1,0:T(8,128)(2,1)S(1)}, u32[]{:S(2)}, u32[]{:S(2)}) collective-permute-start(bf16[4,48,1152]{2,1,0:T(8,128)(2,1)S(1)} %get-tuple-element.222), channel_id=1, source_target_pairs={{0,16},{1,17},{2,18},{3,19},{4,20},{5,21},{6,22},{7,23},{8,24},{9,... | collective-permute-start | bytes 1327112 | tf_op jit(solution)/shard_map/ppermute | solution.py:432
  481.0 27.7 %collective-permute-start.54 = (bf16[4,48,1152]{2,1,0:T(8,128)(2,1)S(1)}, bf16[4,48,1152]{2,1,0:T(8,128)(2,1)S(1)}, u32[]{:S(2)}, u32[]{:S(2)}) collective-permute-start(bf16[4,48,1152]{2,1,0:T(8,128)(2,1)S(1)} %get-tuple-element.220), channel_id=1, source_target_pairs={{0,8},{1,9},{2,10},{3,11},{4,12},{5,13},{6,14},{7,15},{8,0},{9,1},... | collective-permute-start | bytes 1327112 | tf_op jit(solution)/shard_map/ppermute | solution.py:432
  490.9 20.6 %collective-permute-start.67 = (bf16[48,1152]{1,0:T(8,128)(2,1)S(1)}, bf16[48,1152]{1,0:T(8,128)(2,1)S(1)}, u32[]{:S(2)}, u32[]{:S(2)}) collective-permute-start(bf16[48,1152]{1,0:T(8,128)(2,1)S(1)} %get-tuple-element.254), channel_id=1, source_target_pairs={{0,6},{1,7},{2,4},{3,5},{4,2},{5,3},{6,0},{7,1},{8,14},{9,15},{10,... | collective-permute-start | bytes 331784 | tf_op jit(solution)/shard_map/ppermute | solution.py:432
  493.2 20.3 %collective-permute-start.66 = (bf16[48,1152]{1,0:T(8,128)(2,1)S(1)}, bf16[48,1152]{1,0:T(8,128)(2,1)S(1)}, u32[]{:S(2)}, u32[]{:S(2)}) collective-permute-start(bf16[48,1152]{1,0:T(8,128)(2,1)S(1)} %get-tuple-element.255), channel_id=1, source_target_pairs={{0,4},{1,5},{2,6},{3,7},{4,0},{5,1},{6,2},{7,3},{8,12},{9,13},{10,... | collective-permute-start | bytes 331784 | tf_op jit(solution)/shard_map/ppermute | solution.py:432
  (114 other events, 1975.4 us)
Sparse Core Ops, SparseCore 0:
  284.2 117.2 all-reduce.3
